TPU v7x, 32 devices: a whole 2x2x4 slice. The times are simulated.
32 devices in a mesh: dp: 8 (over z, x), pipe: 2 (over y), tensor: 2 (over core).
Axes of the slice: x: 2, y: 2, z: 4, core: 2. Of those that a mesh axis runs over, the one named last changes fastest.
Arguments:
- query_states: bfloat16 [2, 512, 4096], P('pipe', 'dp', 'tensor'), may hold values from -6 to 6
- passage_hidden_states: bfloat16 [2, 1440, 4096], P('pipe', 'dp', 'tensor'), may hold values from -6 to 6
- w_query: bfloat16 [2, 4096, 4096], P('pipe', 'dp', 'tensor'), may hold values from -0.09375 to 0.09375
- key_matrix: bfloat16 [2, 4096, 1024], P('pipe', 'dp', 'tensor'), may hold values from -0.09375 to 0.09375
- value_matrix: bfloat16 [2, 4096, 1024], P('pipe', 'dp', 'tensor'), may hold values from -0.09375 to 0.09375
- w_out: bfloat16 [2, 4096, 4096], P('pipe', 'tensor', 'dp'), may hold values from -0.09375 to 0.09375
- final_gain: bfloat16 [4096], P('tensor'), may hold values from 0.5 to 2
- w_vector: bfloat16 [4096, 128], P('tensor'), may hold values from -0.09375 to 0.09375
- lengths: int32 [8], P('dp'), may hold values from 1 to 180, 896 in all
- teacher: float32 [16, 8], P(('dp', 'pipe')), may hold values from -12 to 12
Outputs:
- boundary_queries: bfloat16 [2, 512, 4096], P('pipe', 'dp', 'tensor')
- boundary_passages: bfloat16 [2, 1440, 4096], P('pipe', 'dp', 'tensor')
- scores: float32 [16, 8], P(('dp', 'pipe'))
- divergence: float32 [16], P(('dp', 'pipe'))
Inputs may be any that keep to these rules, and one draw needn't show every extreme that they name: Each passage's valid tokens come first; slots after lengths[p] are padding. Some passage fills all 180 slots.
All inputs are finite; a program needn't handle non-finite values. No bound on the sum of `lengths` on one device may be relied on, other than what follows from the above.
Results may differ from a plain program's by a relative error of at most 0.0075.
Values may be sent and summed in bfloat16 or wider, within the bound.
A program may use at most 128 MiB of HBM per device.

v0:
```python
import jax
import jax.numpy as jnp
from jax import lax
from jax.sharding import PartitionSpec as P

MODEL_WIDTH = 4096
HEAD_WIDTH = 128
VEC = 128
QLEN = 32
PLEN = 180


norm_epsilon = 1e-05
vector_epsilon = 1e-06
rope_base = 10000.0


def from_root(array, axis, root):
    mine = lax.axis_index(axis) == root
    return lax.psum(jnp.where(mine, array, jnp.zeros_like(array)), axis)


def rotate(values_in, positions):
    half_size = values_in.shape[-1] // 2
    frequency = rope_base ** (-jnp.arange(half_size).astype(jnp.float32) / half_size)
    angles = positions.astype(jnp.float32)[:, None] * frequency[None, :]
    cosine = jnp.cos(angles)[:, None, :]
    sine = jnp.sin(angles)[:, None, :]
    first_half = values_in[..., :half_size]
    second_half = values_in[..., half_size:]
    return jnp.concatenate(
        [first_half * cosine - second_half * sine, second_half * cosine + first_half * sine],
        axis=-1,
    )


def attend(queries, keys, values_in):
    batch_count, length, head_count, head_size = queries.shape
    key_heads = keys.shape[2]
    grouped = queries.reshape(batch_count, length, key_heads, head_count // key_heads, head_size)
    logits = jnp.einsum(
        "bskgd,bukd->bkgsu", grouped, keys, preferred_element_type=jnp.float32
    ) * head_size ** (-0.5)
    causal = jnp.arange(length)[:, None] >= jnp.arange(length)[None, :]
    weights = jnp.where(causal, jnp.exp(logits), 0.0)
    probability = (weights / jnp.sum(weights, axis=-1, keepdims=True)).astype(jnp.bfloat16)
    combined = jnp.einsum(
        "bkgsu,bukd->bskgd", probability, values_in, preferred_element_type=jnp.float32
    )
    return combined.reshape(batch_count * length, head_count * head_size).astype(jnp.bfloat16)


def by_sequence(array_in, head_number, seq_length):
    return array_in.reshape(-1, seq_length, head_number, HEAD_WIDTH)


def late_scores(query_vectors, passage_vectors, passage_lengths):
    sims = jnp.einsum(
        "qtc,psc->qtps", query_vectors, passage_vectors, preferred_element_type=jnp.float32
    )
    valid = jnp.arange(passage_vectors.shape[1])[None, :] < passage_lengths[:, None]
    masked = jnp.where(valid[None, None], sims, -3.0)
    return jnp.sum(jnp.max(masked, axis=3), axis=1)


def body(
    query_states,
    passage_hidden_states,
    w_query,
    key_matrix,
    value_matrix,
    w_out,
    final_gain,
    w_vector,
    lengths,
    teacher,
):
    query_rows = query_states[0]
    passage_rows = passage_hidden_states[0]
    query_count = query_rows.shape[0]
    joined = jnp.concatenate([query_rows, passage_rows], axis=0)
    widened = joined.astype(jnp.float32)
    squares = jnp.sum(widened * widened, axis=1)
    total = lax.psum(squares, "tensor")
    normed_local = (widened * lax.rsqrt(total / MODEL_WIDTH + norm_epsilon)[:, None]).astype(
        jnp.bfloat16
    )
    normed = lax.all_gather(normed_local, "tensor", axis=1, tiled=True)
    query_cols = w_query.shape[2]
    key_cols = key_matrix.shape[2]
    pieces = (
        lax.all_gather(w_query[0], "dp", axis=0, tiled=True),
        lax.all_gather(key_matrix[0], "dp", axis=0, tiled=True),
        lax.all_gather(value_matrix[0], "dp", axis=0, tiled=True),
    )
    queries, keys, unprojected_values = tuple(
        (jnp.dot(normed, piece, preferred_element_type=jnp.float32) for piece in pieces)
    )
    values_out = unprojected_values.astype(jnp.bfloat16)
    query_heads = query_cols // HEAD_WIDTH
    key_heads = key_cols // HEAD_WIDTH
    query_pos = jnp.arange(QLEN)
    passage_pos = jnp.arange(PLEN)
    short_q = rotate(by_sequence(queries[:query_count], query_heads, QLEN), query_pos).astype(
        jnp.bfloat16
    )
    short_k = rotate(by_sequence(keys[:query_count], key_heads, QLEN), query_pos).astype(
        jnp.bfloat16
    )
    short_v = by_sequence(values_out[:query_count], key_heads, QLEN)
    long_q = rotate(by_sequence(queries[query_count:], query_heads, PLEN), passage_pos).astype(
        jnp.bfloat16
    )
    long_k = rotate(by_sequence(keys[query_count:], key_heads, PLEN), passage_pos).astype(
        jnp.bfloat16
    )
    long_v = by_sequence(values_out[query_count:], key_heads, PLEN)
    attended = jnp.concatenate(
        [attend(short_q, short_k, short_v), attend(long_q, long_k, long_v)], axis=0
    )
    branch_full = jnp.dot(
        attended,
        lax.all_gather(w_out[0], "dp", axis=1, tiled=True),
        preferred_element_type=jnp.float32,
    )
    branch = lax.psum_scatter(
        branch_full.astype(jnp.bfloat16), "tensor", scatter_dimension=1, tiled=True
    ).astype(jnp.float32)
    updated = (widened + branch).astype(jnp.bfloat16)
    boundary_queries = updated[:query_count][None]
    boundary_passages = updated[query_count:][None]
    scaled = (updated.astype(jnp.float32) * final_gain.astype(jnp.float32)[None, :]).astype(
        jnp.bfloat16
    )
    partial_vec = jnp.dot(scaled, w_vector, preferred_element_type=jnp.float32)
    projected = lax.psum(partial_vec.astype(jnp.bfloat16), "tensor").astype(jnp.float32)
    vectors = (
        projected
        * lax.rsqrt(jnp.sum(projected * projected, axis=1, keepdims=True) + vector_epsilon)
    ).astype(jnp.bfloat16)
    query_vectors = vectors[:query_count].reshape(-1, QLEN, VEC)
    passage_vectors = vectors[query_count:].reshape(-1, PLEN, VEC)
    last_section = lax.axis_size("pipe") - 1
    query_vectors, passage_vectors = (
        from_root(query_vectors, "pipe", last_section),
        from_root(passage_vectors, "pipe", last_section),
    )
    owned = query_vectors.shape[0] // lax.axis_size("pipe")
    own_queries = lax.dynamic_slice_in_dim(query_vectors, lax.axis_index("pipe") * owned, owned, 0)
    pieces = (
        lax.all_gather(passage_vectors, "dp", axis=0, tiled=True),
        lax.all_gather(lengths, "dp", axis=0, tiled=True),
    )
    block = late_scores(own_queries, pieces[0], pieces[1])
    log_student = block - jnp.log(jnp.sum(jnp.exp(block), axis=1, keepdims=True))
    log_teacher = teacher - jnp.log(jnp.sum(jnp.exp(teacher), axis=1, keepdims=True))
    divergence = jnp.sum(jnp.exp(log_teacher) * (log_teacher - log_student), axis=1)
    return (boundary_queries, boundary_passages, block, divergence)


def solution(mesh):
    in_specs = (
        P("pipe", "dp", "tensor"),
        P("pipe", "dp", "tensor"),
        P("pipe", "dp", "tensor"),
        P("pipe", "dp", "tensor"),
        P("pipe", "dp", "tensor"),
        P("pipe", "tensor", "dp"),
        P("tensor"),
        P("tensor", None),
        P("dp"),
        P(("dp", "pipe"), None),
    )
    out_specs = (
        P("pipe", "dp", "tensor"),
        P("pipe", "dp", "tensor"),
        P(("dp", "pipe"), None),
        P(("dp", "pipe")),
    )
    return jax.shard_map(body, mesh=mesh, in_specs=in_specs, out_specs=out_specs, check_vma=False)
```

profile of v0, /device:TPU:0, one launch (start us, length us, event | category | flops | bytes accessed | tf_op | source)
XLA Modules:
  0.0 714.7 jit_solution(4791329132297808971)
XLA Ops:
  7.2 0.0 all-gather.10.cloned.1.call-start
  7.2 1.5 fusion.12
  8.7 2.6 psum.28
  11.3 2.4 fusion.13
  13.7 0.0 all-gather.14.cloned.1.call-start
  13.8 0.7 all-gather.14.cloned.1.call-update
  14.5 0.0 all-gather.12.cloned.1.call-start
  14.5 0.7 all-gather.12.cloned.1.call-update
  15.2 0.0 all-gather.16.cloned.1.call-start
  15.3 0.5 all-gather.16.cloned.1.call-update
  15.8 0.5 all-gather.18.cloned.1.call-update
  16.4 0.0 reduce-scatter.2.cloned.1.call-start
  16.5 0.1 multiply_cosine_fusion.1
  16.6 0.4 multiply_cosine_fusion
  17.1 9.9 %all-gather.10.cloned.1.call-done = bf16[244,4096]{1,0:T(8,128)(2,1)} async-done(((bf16[244,2048]{1,0:T(8,128)(2,1)}), bf16[244,4096]{1,0:T(8,128)(2,1)}) %all-gather.10.cloned.1.call-update) | async-done | bytes 1998864 | tf_op jit(solution)/shard_map/all_gather | solution.py:88
  26.9 76.7 %all-gather.14.cloned.1.call-done = bf16[1,4096,512]{2,1,0:T(8,128)(2,1)} async-done(((bf16[1,512,512]{2,1,0:T(8,128)(2,1)}), bf16[1,4096,512]{2,1,0:T(8,128)(2,1)}) %all-gather.14.cloned.1.call-update) | async-done | bytes 4194320 | tf_op jit(solution)/shard_map/all_gather | solution.py:93
  103.7 4.0 fusion.7
  107.7 69.8 %all-gather.12.cloned.1.call-done = bf16[1,4096,512]{2,1,0:T(8,128)(2,1)} async-done(((bf16[1,512,512]{2,1,0:T(8,128)(2,1)}), bf16[1,4096,512]{2,1,0:T(8,128)(2,1)}) %all-gather.12.cloned.1.call-update) | async-done | bytes 4194320 | tf_op jit(solution)/shard_map/all_gather | solution.py:94
  177.5 4.0 fusion.27
  181.5 0.1 reshape.284
  181.7 0.7 reshape.283
  182.5 0.1 fusion.65
  182.7 0.3 fusion.64
  182.9 0.1 fusion.44
  183.0 222.4 %all-gather.16.cloned.1.call-done = bf16[1,4096,2048]{2,1,0:T(8,128)(2,1)} async-done(((bf16[1,512,2048]{2,1,0:T(8,128)(2,1)}), bf16[1,4096,2048]{2,1,0:T(8,128)(2,1)}) %all-gather.16.cloned.1.call-update) | async-done | bytes 16777232 | tf_op jit(solution)/shard_map/all_gather | solution.py:92
  405.4 8.6 %fusion.2 = f32[244,2048]{1,0:T(8,128)S(1)} fusion(bf16[244,4096]{1,0:T(8,128)(2,1)} %all-gather.10.cloned.1.call-done, bf16[1,4096,2048]{2,1,0:T(8,128)(2,1)} %all-gather.16.cloned.1.call-done), kind=kOutput, calls=%fused_computation.2 | convolution fusion | flops 4093640704 | bytes 20774912 | tf_op jit(solution)/shard_map/dot_general | solution.py:97
  414.0 0.1 slice.83
  414.2 0.3 copy.69
  414.4 0.1 slice_bitcast_fusion
  414.5 0.7 subtract_convert_fusion
  415.2 0.2 copy.49
  415.4 0.2 copy.50
  415.7 1.3 fusion.11
  417.0 1.0 fusion.21
  418.0 0.3 copy.53
  418.3 1.3 convert_element_type.173
  419.6 0.1 copy.68
  419.7 0.2 subtract_convert_fusion.1
  420.0 0.1 copy.42
  420.0 0.1 copy.43
  420.1 0.6 fusion.26
  420.7 0.3 fusion.30
  421.0 0.1 copy.46
  421.2 0.2 convert_element_type.167
  421.4 211.9 %all-gather.18.cloned.1.call-done = bf16[1,2048,4096]{2,1,0:T(8,128)(2,1)} async-done(((bf16[1,2048,512]{2,1,0:T(8,128)(2,1)}), bf16[1,2048,4096]{2,1,0:T(8,128)(2,1)}) %all-gather.18.cloned.1.call-update) | async-done | bytes 16777232 | tf_op jit(solution)/shard_map/all_gather | solution.py:123
  633.2 11.6 %fusion.4 = bf16[244,4096]{1,0:T(8,128)(2,1)} fusion(bf16[1,2048,4096]{2,1,0:T(8,128)(2,1)} %all-gather.18.cloned.1.call-done, bf16[180,2048]{1,0:T(8,128)(2,1)S(1)} %copy-done.3, bf16[64,2048]{1,0:T(8,128)(2,1)S(1)} %convert_element_type.167), kind=kOutput, calls=%fused_computation.4 | convolution fusion | flops 4096638976 | bytes 19775488 | tf_op jit(solution)/shard_map/dot_general | solution.py:121
  645.7 0.6 dynamic-slice
  646.2 0.8 dynamic-update-slice
  647.0 9.5 %all-reduce = s32[8]{0:T(128)S(1)} all-reduce(s32[8]{0:T(128)S(1)} %dynamic-update-slice), channel_id=1, replica_groups=mesh['dp'=8,'pipe'=2,'tensor'=2] {'dp'}, use_global_device_ids=true, to_apply=%add | all-reduce | flops 8 | bytes 64
  656.5 0.6 exponential_reduce_fusion.1
  657.8 0.1 iota_compare_fusion.2
  657.9 1.6 fusion.14
  659.5 0.4 convolution_convert_fusion.1
  659.9 3.6 psum.29
  663.5 0.1 fusion.49
  663.6 0.1 fusion.50
  663.8 0.9 slice_bitcast_fusion.1
  664.7 0.7 slice_bitcast_fusion.3
  665.4 8.8 %all-reduce.1 = (bf16[1,180,128]{2,1,0:T(8,128)(2,1)S(1)}, bf16[2,32,128]{2,1,0:T(8,128)(2,1)S(1)}) all-reduce(bf16[1,180,128]{2,1,0:T(8,128)(2,1)S(1)} %fusion.54, bf16[2,32,128]{2,1,0:T(8,128)(2,1)S(1)} %bitcast.117), channel_id=1, replica_groups=mesh['dp'=8,'pipe'=2,'tensor'=2] {'pipe'}, use_global_device_ids=true, to_apply=%region_8.9 | all-reduce | flops 31232 | bytes 124928 | tf_op jit(solution)/shard_map/psum | solution.py:20
  674.2 31.2 %all_gather.27 = bf16[8,180,128]{2,1,0:T(8,128)(2,1)S(1)} all-gather(bf16[1,180,128]{2,1,0:T(8,128)(2,1)S(1)} %get-tuple-element.4), channel_id=1, replica_groups=mesh['dp'=8,'pipe'=2,'tensor'=2] {'dp'}, dimensions={0}, use_global_device_ids=true | all-gather | bytes 414720 | tf_op jit(solution)/shard_map/all_gather | solution.py:151
  705.4 0.4 fusion.31
  705.8 0.1 reduce_sum.80
  705.9 0.6 exponential_reduce_fusion
  707.2 0.6 multiply_reduce_fusion
  (41 shorter events, 0.4 us)
Async XLA Ops:
  7.2 652.3 %copy-start = (bf16[2048,128]{1,0:T(8,128)(2,1)S(1)}, bf16[2048,128]{1,0:T(8,128)(2,1)}, u32[]{:S(2)}) copy-start(bf16[2048,128]{1,0:T(8,128)(2,1)} %param.17) | copy-start | bytes 1572868
  7.2 19.8 %all-gather.10.cloned.1.call-start = ((), (), s32[]{:S(2)}) async-start(), calls=%async_computation.1 | async-start | bytes 3047424 | tf_op jit(solution)/shard_map/all_gather | solution.py:88
  13.7 89.9 %all-gather.14.cloned.1.call-start = ((), (), s32[]{:S(2)}) async-start(), calls=%async_computation.4 | async-start | bytes 4718592 | tf_op jit(solution)/shard_map/all_gather | solution.py:93
  14.5 163.0 %all-gather.12.cloned.1.call-start = ((), (), s32[]{:S(2)}) async-start(), calls=%async_computation.3 | async-start | bytes 4718592 | tf_op jit(solution)/shard_map/all_gather | solution.py:94
  15.2 390.2 %all-gather.16.cloned.1.call-start = ((), (), s32[]{:S(2)}) async-start(), calls=%async_computation.5 | async-start | bytes 18874368 | tf_op jit(solution)/shard_map/all_gather | solution.py:92
  15.8 617.5 %all-gather.18.cloned.1.call-start = ((), (), s32[]{:S(2)}) async-start(), calls=%async_computation.6 | async-start | bytes 18874368 | tf_op jit(solution)/shard_map/all_gather | solution.py:123
  16.4 641.5 %reduce-scatter.2.cloned.1.call-start = ((), (), s32[]{:S(2)}) async-start(), calls=%async_computation.2 | async-start | bytes 3047424 | tf_op jit(solution)/shard_map/reduce_scatter | solution.py:126
  415.6 1.3 copy-start.4
  420.1 213.1 %copy-start.3 = (bf16[180,2048]{1,0:T(8,128)(2,1)S(1)}, bf16[180,2048]{1,0:T(8,128)(2,1)}, u32[]{:S(2)}) copy-start(bf16[180,2048]{1,0:T(8,128)(2,1)} %convert_element_type.173) | copy-start | bytes 2211844
  644.9 0.8 copy-start.8
  644.9 11.6 %copy-start.5 = (bf16[2048]{0:T(1024)(128)(2,1)S(1)}, bf16[2048]{0:T(1024)(128)(2,1)}, u32[]{:S(2)}) copy-start(bf16[2048]{0:T(1024)(128)(2,1)} %param.16) | copy-start | bytes 12292
  644.9 11.6 %copy-start.7 = (f32[1,8]{1,0:T(1,128)S(1)}, f32[1,8]{1,0:T(1,128)}, u32[]{:S(2)}) copy-start(f32[1,8]{1,0:T(1,128)} %param.19) | copy-start | bytes 100
  644.9 13.0 %copy-start.1 = (bf16[1,180,2048]{2,1,0:T(8,128)(2,1)S(1)}, bf16[1,180,2048]{2,1,0:T(8,128)(2,1)}, u32[]{:S(2)}) copy-start(bf16[1,180,2048]{2,1,0:T(8,128)(2,1)} %param.11) | copy-start | bytes 2211844
  644.9 13.0 %copy-start.2 = (bf16[1,64,2048]{2,1,0:T(8,128)(2,1)S(1)}, bf16[1,64,2048]{2,1,0:T(8,128)(2,1)}, u32[]{:S(2)}) copy-start(bf16[1,64,2048]{2,1,0:T(8,128)(2,1)} %param.10) | copy-start | bytes 786436
  705.9 1.9 copy-start.6
Sparse Core Ops, SparseCore 0:
  13.8 13.0 all-gather.9
  29.1 74.5 all-gather.13
  105.8 71.6 all-gather.11
  179.5 225.8 all-gather.15
  407.3 225.9 all-gather.17
  645.0 7.7 reduce-scatter.1
where the time goes:
time: 715 us
  waiting for transfers between devices  593 us (83%)
  blocking collectives  55.6 us (8%)
  matrix products  32.3 us (5%)
  between operations  16.6 us (2%)
  other arithmetic  9.36 us (1%)
  local copies, waits for them, and re-layouts  7.48 us (1%)
    all_gather x1, waiting for transfers between devices, body(): lax.all_gather(w_query[0], 'dp', axis=0, tiled=True)  222 us
    all_gather x1, waiting for transfers between devices, body(): lax.all_gather(w_out[0], 'dp', axis=1, tiled=True)  212 us
    all_gather x1, waiting for transfers between devices, body(): lax.all_gather(key_matrix[0], 'dp', axis=0, tiled=True)  76.7 us
    all_gather x1, waiting for transfers between devices, body(): lax.all_gather(value_matrix[0], 'dp', axis=0, tiled=True)  69.8 us
    all_gather x1, blocking collectives, body(): lax.all_gather(passage_vectors, 'dp', axis=0, tiled=True)  31.2 us
    dot_general x3, matrix products, body(): jnp.dot(normed, piece, preferred_element_type=jnp.float32)  16.7 us
  transfers between devices with their start and end apart: 6, of which 5 were waited for; matrix products, arithmetic and copies ran while one was open for 4% of the time, Pallas kernels for 0%

commit v1 on v0

--- a/solution.py
+++ b/solution.py
@@ -1,6 +1,9 @@
 import jax
 import jax.numpy as jnp
+import numpy as np
 from jax import lax
+from jax.experimental import pallas as pl
+from jax.experimental.pallas import tpu as pltpu
 from jax.sharding import PartitionSpec as P
 
 MODEL_WIDTH = 4096
@@ -158,6 +161,439 @@
     return (boundary_queries, boundary_passages, block, divergence)
 
 
+ROWS = 256
+Q_ROWS = 64
+MESH = pl.DeviceIdType.MESH
+
+
+def remote(src, dst, send, recv, device):
+    return pltpu.make_async_remote_copy(
+        src_ref=src, dst_ref=dst, send_sem=send, recv_sem=recv, device_id=device, device_id_type=MESH
+    )
+
+
+def greet(devices):
+    barrier = pltpu.get_barrier_semaphore()
+    for device in devices:
+        pl.semaphore_signal(barrier, inc=1, device_id=device, device_id_type=MESH)
+    pl.semaphore_wait(barrier, len(devices))
+
+
+def place():
+    dp = lax.axis_index("dp")
+    return dp // 2, lax.rem(dp, 2), lax.axis_index("tensor")
+
+
+class Line:
+    def __init__(self, own, held, send, recv, z, x):
+        self.own, self.held, self.send_sem, self.recv_sem, self.z, self.x = own, held, send, recv, z, x
+
+    def copies(self, step):
+        z, x = self.z, self.x
+        up_block = jnp.maximum(z - step, 0)
+        down_block = jnp.minimum(z + step, 3)
+        src_up = self.own if step == 0 else self.held(up_block)
+        src_down = self.own if step == 0 else self.held(down_block)
+        up = remote(
+            src_up, self.held(up_block), self.send_sem.at[0, step], self.recv_sem.at[up_block],
+            {"dp": jnp.minimum(z + 1, 3) * 2 + x},
+        )
+        down = remote(
+            src_down, self.held(down_block), self.send_sem.at[1, step], self.recv_sem.at[down_block],
+            {"dp": jnp.maximum(z - 1, 0) * 2 + x},
+        )
+        return ((z < 3) & (z >= step), up), ((z > 0) & (z + step <= 3), down)
+
+    def send(self, step):
+        for condition, copy in self.copies(step):
+            pl.when(condition)(copy.start)
+
+    def receive(self, step, then=None):
+        for condition, block in ((self.z - 1 - step >= 0, self.z - 1 - step), (self.z + 1 + step <= 3, self.z + 1 + step)):
+
+            @pl.when(condition)
+            def _(block=block):
+                ref = self.held(block)
+                remote(ref, ref, self.send_sem.at[0, 0], self.recv_sem.at[block], {"dp": self.x}).wait_recv()
+                if then is not None:
+                    then(block)
+
+    def finish(self):
+        for step in range(3):
+            for condition, copy in self.copies(step):
+                pl.when(condition)(copy.wait_send)
+
+
+def gather_kernel(
+    x_ref, w_ref, wo_ref, xg, wg, wog,
+    local_sem, line_send, line_recv, core_send, core_recv, w_send, w_recv, wx_send, wx_recv, wo_send, wo_recv,
+):
+    z, x, t = place()
+    d = z * 2 + x
+    side = {"dp": z * 2 + 1 - x}
+    partner = {"tensor": 1 - t}
+    others = [lax.rem(z + o, 4) for o in range(4)]
+    greet([{"dp": others[o] * 2 + x} for o in (1, 2, 3)] + [side, partner])
+
+    line = Line(x_ref, lambda b: xg.at[b, t], line_send, line_recv, z, x)
+
+    def w_copy(o):
+        return remote(w_ref.at[others[o]], wg.at[d], w_send.at[o], w_recv.at[o], {"dp": others[o] * 2 + x})
+
+    def side_copy(o):
+        origin = lax.rem(z + 4 - o, 4)
+        slot = wg.at[origin * 2 + x]
+        return remote(w_ref.at[z] if o == 0 else slot, slot, wx_send.at[o], wx_recv.at[o], side)
+
+    def core_copy(block, own=False):
+        slot = xg.at[block, t]
+        return remote(x_ref if own else slot, slot, core_send.at[block], core_recv.at[block], partner)
+
+    def w_receive(o):
+        origin = lax.rem(z + 4 - o, 4)
+        slot = wg.at[origin * 2 + x]
+        remote(slot, slot, w_send.at[o], w_recv.at[o], side).wait_recv()
+        side_copy(o).start()
+
+    wo_copy = remote(wo_ref, wog.at[x], wo_send, wo_recv, side)
+    side_copy(0).start()
+    line.send(0)
+    for o in (1, 3, 2):
+        w_copy(o).start()
+    core_copy(z, own=True).start()
+    locals_ = [
+        pltpu.make_async_copy(x_ref, xg.at[z, t], local_sem.at[0]),
+        pltpu.make_async_copy(w_ref.at[z], wg.at[d], local_sem.at[1]),
+        pltpu.make_async_copy(wo_ref, wog.at[x], local_sem.at[2]),
+    ]
+    for copy in locals_:
+        copy.start()
+    forward = lambda block: core_copy(block).start()
+    line.receive(0, forward)
+    line.send(1)
+    w_receive(1)
+    w_receive(3)
+    wo_copy.start()
+    line.receive(1, forward)
+    line.send(2)
+    w_receive(2)
+    line.receive(2, forward)
+    for o in range(4):
+        origin = lax.rem(z + 4 - o, 4)
+        slot = wg.at[origin * 2 + 1 - x]
+        remote(slot, slot, wx_send.at[o], wx_recv.at[o], side).wait_recv()
+    for block in range(4):
+        slot = xg.at[block, 1 - t]
+        remote(slot, slot, core_send.at[block], core_recv.at[block], partner).wait_recv()
+    remote(wog.at[1 - x], wog.at[1 - x], wo_send, wo_recv, side).wait_recv()
+    for copy in locals_:
+        copy.wait()
+    line.finish()
+    for o in (1, 2, 3):
+        w_copy(o).wait_send()
+    for o in range(4):
+        side_copy(o).wait_send()
+        core_copy(o).wait_send()
+    wo_copy.wait_send()
+
+
+def gather(x_block, w_parts, w_out):
+    dma = pltpu.SemaphoreType.DMA
+    any_spec = pl.BlockSpec(memory_space=pl.ANY)
+    return pl.pallas_call(
+        gather_kernel,
+        out_shape=(
+            jax.ShapeDtypeStruct((4, 2) + x_block.shape, x_block.dtype),
+            jax.ShapeDtypeStruct((8,) + w_parts.shape[1:], w_parts.dtype),
+            jax.ShapeDtypeStruct((2,) + w_out.shape, w_out.dtype),
+        ),
+        in_specs=[any_spec] * 3,
+        out_specs=(any_spec,) * 3,
+        scratch_shapes=[
+            dma((3,)), dma((2, 3)), dma((4,)), dma((4,)), dma((4,)),
+            dma((4,)), dma((4,)), dma((4,)), dma((4,)), dma, dma,
+        ],
+        compiler_params=pltpu.CompilerParams(collective_id=1, has_side_effects=True),
+        name="gather",
+    )(x_block, w_parts, w_out)
+
+
+def attention_kernel(x_ref, w_ref, cos_ref, sin_ref, out_ref):
+    half = x_ref.shape[3]
+    first, second = x_ref[0, 0], x_ref[0, 1]
+    raw = jnp.dot(first, w_ref[:half], preferred_element_type=jnp.float32) + jnp.dot(
+        second, w_ref[half:], preferred_element_type=jnp.float32
+    )
+    a, b = first.astype(jnp.float32), second.astype(jnp.float32)
+    total = jnp.sum(a * a, axis=1, keepdims=True) + jnp.sum(b * b, axis=1, keepdims=True)
+    raw = raw * lax.rsqrt(total / (2 * half) + norm_epsilon)
+    cosine, sine = cos_ref[...], sin_ref[...]
+    row = lax.broadcasted_iota(jnp.int32, (ROWS, ROWS), 0)
+    col = lax.broadcasted_iota(jnp.int32, (ROWS, ROWS), 1)
+    start = jnp.where(row < QLEN, 0, jnp.where(row < 2 * QLEN, QLEN, Q_ROWS))
+    seen = (row >= col) & (col >= start)
+
+    def turned(head):
+        part = raw[:, head * HEAD_WIDTH : (head + 1) * HEAD_WIDTH]
+        swapped = jnp.concatenate([part[:, HEAD_WIDTH // 2 :], part[:, : HEAD_WIDTH // 2]], axis=1)
+        return (part * cosine + swapped * sine).astype(jnp.bfloat16)
+
+    heads = raw.shape[1] // HEAD_WIDTH - 2
+    key = turned(heads)
+    value = raw[:, (heads + 1) * HEAD_WIDTH :].astype(jnp.bfloat16)
+    for head in range(heads):
+        logits = lax.dot_general(
+            turned(head), key, (((1,), (1,)), ((), ())), preferred_element_type=jnp.float32
+        ) * HEAD_WIDTH ** (-0.5)
+        weights = jnp.where(seen, jnp.exp(logits), 0.0)
+        probability = (weights / jnp.sum(weights, axis=1, keepdims=True)).astype(jnp.bfloat16)
+        out_ref[0, :, head * HEAD_WIDTH : (head + 1) * HEAD_WIDTH] = jnp.dot(
+            probability, value, preferred_element_type=jnp.float32
+        ).astype(jnp.bfloat16)
+
+
+def attention(xg, weights, cosine, sine):
+    heads_cols = weights.shape[1] - 2 * HEAD_WIDTH
+    return pl.pallas_call(
+        attention_kernel,
+        grid=(4,),
+        out_shape=jax.ShapeDtypeStruct((4, ROWS, heads_cols), jnp.bfloat16),
+        in_specs=[
+            pl.BlockSpec((1,) + xg.shape[1:], lambda i: (i, 0, 0, 0)),
+            pl.BlockSpec(weights.shape, lambda i: (0, 0)),
+            pl.BlockSpec(cosine.shape, lambda i: (0, 0)),
+            pl.BlockSpec(sine.shape, lambda i: (0, 0)),
+        ],
+        out_specs=pl.BlockSpec((1, ROWS, heads_cols), lambda i: (i, 0, 0)),
+        compiler_params=pltpu.CompilerParams(vmem_limit_bytes=48 << 20),
+        name="attention",
+    )(xg, weights, cosine, sine)
+
+
+def output_kernel(
+    a_ref, wo_ref, x_ref, gain_ref, wv_ref, updated_ref, partial_ref,
+    ag, term, other, total, branch,
+    line_send, line_recv, core_send, core_recv, row_send, row_recv,
+):
+    z, x, t = place()
+    partner = {"tensor": 1 - t}
+    peers = [{"dp": lax.rem(z + o, 4) * 2 + x, "tensor": lax.rem(t + c, 2)} for o in range(4) for c in range(2)]
+    greet(peers[1:])
+    line = Line(a_ref, lambda b: ag.at[b], line_send, line_recv, z, x)
+    line.send(0)
+    ag[pl.ds(z, 1)] = a_ref[...][None]
+    line.receive(0)
+    line.send(1)
+    line.receive(1)
+    line.send(2)
+    line.receive(2)
+
+    half = ROWS // 2
+    depth = a_ref.shape[2]
+    cols = wo_ref.shape[2]
+    group = z // 2
+    parity = lax.rem(z, 2)
+
+    def core_copy(o, rb):
+        return remote(term.at[o, 1 - t], other.at[o], core_send.at[o], core_recv.at[o], partner)
+
+    def row_copy(o, rb):
+        return remote(
+            total.at[o], branch.at[parity, t], row_send.at[o], row_recv.at[parity, t],
+            {"dp": rb * 2 + x, "tensor": group},
+        )
+
+    blocks = [lax.rem(z + o, 4) for o in (1, 2, 3, 0)]
+    for o, rb in enumerate(blocks):
+        for side in range(2):
+            acc = jnp.zeros((ROWS, cols), jnp.float32)
+            for part in range(4):
+                acc += jnp.dot(
+                    ag[part, rb], wo_ref[side, part * depth : (part + 1) * depth],
+                    preferred_element_type=jnp.float32,
+                )
+            rounded = acc.astype(jnp.bfloat16)
+            term[o, 0, :, side * cols : (side + 1) * cols] = rounded[:half]
+            term[o, 1, :, side * cols : (side + 1) * cols] = rounded[half:]
+        core_copy(o, rb).start()
+    mine = t == group
+    for o, rb in enumerate(blocks):
+        core_copy(o, rb).wait_recv()
+        summed = term[o, t].astype(jnp.float32) + other[o].astype(jnp.float32)
+        total[o] = summed.astype(jnp.bfloat16)
+        if o < 3:
+            row_copy(o, rb).start()
+        else:
+            pl.when(jnp.logical_not(mine))(row_copy(o, rb).start)
+
+            @pl.when(mine)
+            def _():
+                branch[parity, t] = total[o]
+
+    for p in range(2):
+        for h in range(2):
+            own_piece = mine & (parity == p) & (t == h)
+
+            @pl.when(jnp.logical_not(own_piece))
+            def _(p=p, h=h):
+                slot = branch.at[p, h]
+                remote(slot, slot, row_send.at[0], row_recv.at[p, h], partner).wait_recv()
+
+    width = 2 * cols
+    for h in range(2):
+        rows = slice(h * half, (h + 1) * half)
+        partial = jnp.zeros((half, VEC), jnp.float32)
+        for p in range(2):
+            columns = slice(p * width, (p + 1) * width)
+            updated = (
+                x_ref[rows, columns].astype(jnp.float32) + branch[p, h].astype(jnp.float32)
+            ).astype(jnp.bfloat16)
+            updated_ref[rows, columns] = updated
+            scaled = (updated.astype(jnp.float32) * gain_ref[:, columns]).astype(jnp.bfloat16)
+            partial += jnp.dot(scaled, wv_ref[columns], preferred_element_type=jnp.float32)
+        partial_ref[rows] = partial.astype(jnp.bfloat16)
+    line.finish()
+    for o, rb in enumerate(blocks):
+        core_copy(o, rb).wait_send()
+        if o < 3:
+            row_copy(o, rb).wait_send()
+        else:
+            pl.when(jnp.logical_not(mine))(row_copy(o, rb).wait_send)
+
+
+def output(attended, wog, x_block, gain, w_vector):
+    dma = pltpu.SemaphoreType.DMA
+    bf16 = jnp.bfloat16
+    cols = 2 * wog.shape[2]
+    vmem = pl.BlockSpec(memory_space=pltpu.VMEM)
+    return pl.pallas_call(
+        output_kernel,
+        out_shape=(
+            jax.ShapeDtypeStruct(x_block.shape, bf16),
+            jax.ShapeDtypeStruct((ROWS, VEC), bf16),
+        ),
+        in_specs=[vmem] * 5,
+        out_specs=(vmem,) * 2,
+        scratch_shapes=[
+            pltpu.VMEM((4,) + attended.shape, bf16),
+            pltpu.VMEM((4, 2, ROWS // 2, cols), bf16),
+            pltpu.VMEM((4, ROWS // 2, cols), bf16),
+            pltpu.VMEM((4, ROWS // 2, cols), bf16),
+            pltpu.VMEM((2, 2, ROWS // 2, cols), bf16),
+            dma((2, 3)), dma((4,)), dma((4,)), dma((4,)), dma((4,)), dma((2, 2)),
+        ],
+        compiler_params=pltpu.CompilerParams(
+            collective_id=2, has_side_effects=True, vmem_limit_bytes=48 << 20
+        ),
+        name="output",
+    )(attended, wog, x_block, gain, w_vector)
+
+
+def vector_kernel(part_ref, valid_ref, all_ref, other, mine_buf, core_send, core_recv, send, recv):
+    dp, pipe, t = lax.axis_index("dp"), lax.axis_index("pipe"), lax.axis_index("tensor")
+    partner = {"tensor": 1 - t}
+    ring = [lax.rem(dp + o, 8) for o in range(8)]
+    pairs = [(o, p) for o in range(8) for p in range(2)][1:]
+    targets = [{"dp": ring[o], "pipe": lax.rem(pipe + p, 2)} for o, p in pairs]
+    greet([partner] + targets)
+    exchange = remote(part_ref, other, core_send, core_recv, partner)
+    exchange.start()
+    exchange.wait_recv()
+    projected = part_ref[...].astype(jnp.float32) + other[...].astype(jnp.float32)
+    vectors = projected * lax.rsqrt(jnp.sum(projected * projected, axis=1, keepdims=True) + vector_epsilon)
+    vectors = jnp.where(valid_ref[...] > 0.5, vectors, vectors[Q_ROWS : Q_ROWS + 1])
+    mine_buf[...] = vectors.astype(jnp.bfloat16)
+
+    def push(index):
+        return remote(mine_buf, all_ref.at[dp], send.at[index], recv.at[dp], targets[index])
+
+    @pl.when(pipe == 1)
+    def _():
+        for index in range(15):
+            push(index).start()
+        all_ref[pl.ds(dp, 1)] = mine_buf[...][None]
+
+    for o in range(8):
+        slot = all_ref.at[ring[o]]
+        wait = remote(slot, slot, send.at[0], recv.at[ring[o]], partner).wait_recv
+        if o == 0:
+            pl.when(pipe == 0)(wait)
+        else:
+            wait()
+    exchange.wait_send()
+
+    @pl.when(pipe == 1)
+    def _():
+        for index in range(15):
+            push(index).wait_send()
+
+
+def share_vectors(partial, valid):
+    dma = pltpu.SemaphoreType.DMA
+    vmem = pl.BlockSpec(memory_space=pltpu.VMEM)
+    return pl.pallas_call(
+        vector_kernel,
+        out_shape=jax.ShapeDtypeStruct((8, ROWS, VEC), jnp.bfloat16),
+        in_specs=[vmem] * 2,
+        out_specs=vmem,
+        scratch_shapes=[
+            pltpu.VMEM((ROWS, VEC), jnp.bfloat16),
+            pltpu.VMEM((ROWS, VEC), jnp.bfloat16),
+            dma, dma, dma((15,)), dma((8,)),
+        ],
+        compiler_params=pltpu.CompilerParams(collective_id=3, has_side_effects=True),
+        name="share_vectors",
+    )(partial, valid)
+
+
+def rope_tables():
+    position = np.concatenate([np.arange(QLEN), np.arange(QLEN), np.arange(ROWS - Q_ROWS)])
+    half = HEAD_WIDTH // 2
+    frequency = np.float32(rope_base) ** (-np.arange(half, dtype=np.float32) / np.float32(half))
+    angles = position.astype(np.float32)[:, None] * frequency[None, :]
+    cosine, sine = np.cos(angles), np.sin(angles)
+    return (
+        jnp.asarray(np.concatenate([cosine, cosine], axis=1), jnp.float32),
+        jnp.asarray(np.concatenate([-sine, sine], axis=1), jnp.float32),
+    )
+
+
+def by_heads(
+    query_states, passage_hidden_states, w_query, key_matrix, value_matrix, w_out,
+    final_gain, w_vector, lengths, teacher,
+):
+    x_block = jnp.concatenate(
+        [query_states[0], jnp.pad(passage_hidden_states[0], ((0, ROWS - Q_ROWS - PLEN), (0, 0)))], axis=0
+    )
+    depth = w_query.shape[1]
+    w_parts = jnp.concatenate(
+        [array[0].reshape(depth, 4, -1).transpose(1, 0, 2) for array in (w_query, key_matrix, value_matrix)],
+        axis=2,
+    )
+    xg, wg, wog = gather(x_block, w_parts, w_out[0])
+    cosine, sine = rope_tables()
+    attended = attention(xg, wg.reshape(-1, wg.shape[2]), cosine, sine)
+    updated, partial = output(
+        attended, wog, x_block, final_gain.astype(jnp.float32)[None, :], w_vector
+    )
+    slot = jnp.arange(ROWS) - Q_ROWS
+    valid = jnp.broadcast_to((slot < lengths[0])[:, None], (ROWS, VEC)).astype(jnp.float32)
+    vectors = share_vectors(partial, valid)
+    dp, pipe = lax.axis_index("dp"), lax.axis_index("pipe")
+    own = lax.dynamic_slice(vectors, (dp, pipe * QLEN, 0), (1, QLEN, VEC))[0]
+    sims = jnp.einsum("tc,psc->tps", own, vectors[:, Q_ROWS:], preferred_element_type=jnp.float32)
+    block = jnp.sum(jnp.max(sims, axis=2), axis=0)[None]
+    log_student = block - jnp.log(jnp.sum(jnp.exp(block), axis=1, keepdims=True))
+    log_teacher = teacher - jnp.log(jnp.sum(jnp.exp(teacher), axis=1, keepdims=True))
+    divergence = jnp.sum(jnp.exp(log_teacher) * (log_teacher - log_student), axis=1)
+    return (
+        updated[None, :Q_ROWS],
+        updated[None, Q_ROWS : Q_ROWS + PLEN],
+        block,
+        divergence,
+    )
+
+
 def solution(mesh):
     in_specs = (
         P("pipe", "dp", "tensor"),
@@ -177,4 +613,7 @@
         P(("dp", "pipe"), None),
         P(("dp", "pipe")),
     )
-    return jax.shard_map(body, mesh=mesh, in_specs=in_specs, out_specs=out_specs, check_vma=False)
+    small = dict(mesh.shape) == {"dp": 8, "pipe": 2, "tensor": 2}
+    return jax.shard_map(
+        by_heads if small else body, mesh=mesh, in_specs=in_specs, out_specs=out_specs, check_vma=False
+    )

time: 715 us -> 329 us (0.46)
  waiting for transfers between devices: 593 us -> 0 us
  Pallas kernels: 0 us -> 299 us
  blocking collectives: 55.6 us -> 0 us
  matrix products: 32.3 us -> 1.44 us
  between operations: 16.6 us -> 2.86 us
    all_gather x5 -> x0, waiting for transfers between devices: 591 us -> none  [the longest x1 222 us: body(): lax.all_gather(w_query[0], 'dp', axis=0, tiled=True)]
    pallas_call x0 -> x4, Pallas kernels: none -> 299 us  [the longest x1 145 us: gather(): pl.pallas_call(gather_kernel, out_shape=(jax.ShapeDtypeStruct((4, 2) + x_...]
    all_gather x1 -> x0, blocking collectives: 31.2 us -> none  [body(): lax.all_gather(passage_vectors, 'dp', axis=0, tiled=True)]
    dot_general x10 -> x1, matrix products: 32.3 us -> 1.44 us  [by_heads(): jnp.einsum('tc,psc->tps', own, vectors[:, Q_ROWS:], preferred_element_typ...]
    psum x3 -> x0, blocking collectives: 15 us -> none  [the longest x1 8.79 us: from_root(): return lax.psum(jnp.where(mine, array, jnp.zeros_like(array)), axis)]
    unnamed x1 -> x0, blocking collectives: 9.46 us -> none
  transfers between devices with their start and end apart: 6 -> 0, of which waited for: 5 -> 0; matrix products, arithmetic and copies ran while one was open for 4% -> 0% of each run, Pallas kernels for 0% -> 0%
where the time goes in v1:
time: 329 us; the launch traced here: 323 us
  Pallas kernels  299 us (91%)
  local copies, waits for them, and re-layouts  13.7 us (4%)
  other arithmetic  6.2 us (2%)
    pallas_call x1, Pallas kernels, gather(): pl.pallas_call(gather_kernel, out_shape=(jax.ShapeDtypeStruct((4, 2) + x_...  145 us
    pallas_call x1, Pallas kernels, output(): pl.pallas_call(output_kernel, out_shape=(jax.ShapeDtypeStruct(x_block.sha...  111 us
    pallas_call x1, Pallas kernels, share_vectors(): pl.pallas_call(vector_kernel, out_shape=jax.ShapeDtypeStruct((8, ROWS, VE...  25.3 us
    pallas_call x1, Pallas kernels, attention(): pl.pallas_call(attention_kernel, grid=(4,), out_shape=jax.ShapeDtypeStruc...  17.5 us
    unnamed x21, local copies, waits for them, and re-layouts  6.86 us

profile of v1, /device:TPU:0, one launch (start us, length us, event | category | flops | bytes accessed | tf_op | source)
XLA Modules:
  0.0 323.1 jit_solution(12807112125184982172)
XLA Ops:
  0.6 2.3 fusion.1.x_ref
  2.9 3.9 %copy.22 = bf16[1,512,2048]{1,2,0:T(8,128)(2,1)} copy(bf16[1,512,2048]{2,1,0:T(8,128)(2,1)} %param.14) | data formatting | bytes 4194304 | tf_op args[2]
  6.9 0.0 copy-start.5
  6.9 2.8 copy.23
  9.7 0.0 copy-done.5
  9.7 0.2 copy.24
  10.0 0.3 copy.25
  10.2 2.1 copy.26
  12.3 1.3 copy.27
  13.6 1.9 pad_maximum_fusion.w_ref
  15.5 0.0 copy-start.2
  15.5 0.0 copy-start.3
  15.5 144.9 %gather.1 = (bf16[4,2,256,2048]{3,2,1,0:T(8,128)(2,1)}, bf16[8,512,768]{2,1,0:T(8,128)(2,1)}, bf16[2,2048,512]{2,1,0:T(8,128)(2,1)}) custom-call(bf16[256,2048]{1,0:T(8,128)(2,1)} %fusion.1.x_ref, bf16[4,512,768]{2,1,0:T(8,128)(2,1)} %pad_maximum_fusion.w_ref, bf16[2048,512]{1,0:T(8,128)(2,1)} %bitcast.28), custom_call_target="tpu_custom_call" | custom-call | tf_op jit(solution)/shard_map/gather/pallas_call | solution.py:303
  160.5 0.0 copy-done.2
  160.5 0.0 copy-done.3
  160.5 0.0 copy-start.6
  160.5 0.0 copy-start
  160.5 0.0 copy-start.1
  160.5 17.5 %attention.1.a_ref = bf16[4,256,512]{2,1,0:T(8,128)(2,1)S(1)} custom-call(bf16[4,2,256,2048]{3,2,1,0:T(8,128)(2,1)} %get-tuple-element.9.x_ref, bf16[4096,768]{1,0:T(8,128)(2,1)} %bitcast.27, f32[256,128]{1,0:T(8,128)S(1)} %copy-done.2, f32[256,128]{1,0:T(8,128)S(1)} %copy-done.3), custom_call_target="tpu_custom_call" | custom-call | tf_op jit(solution)/shard_map/attention/pallas_call | solution.py:357
  178.0 0.0 copy-done.6
  178.1 0.0 copy-done
  178.1 0.0 copy-done.1
  178.1 0.0 copy-start.8
  178.1 111.2 %output.1 = (bf16[256,2048]{1,0:T(8,128)(2,1)S(1)}, bf16[256,128]{1,0:T(8,128)(2,1)S(1)}) custom-call(bf16[4,256,512]{2,1,0:T(8,128)(2,1)S(1)} %attention.1.a_ref, bf16[2,2048,512]{2,1,0:T(8,128)(2,1)} %get-tuple-element.11.wo_ref, bf16[256,2048]{1,0:T(8,128)(2,1)S(1)} %copy-done, f32[1,2048]{1,0:T(1,128)S(1)} %bitcast.24, bf16[2048,128]{1,0:T(8,128)(2,1)S(1)} %copy-done.1), custom_call_target="tpu_custom_call" | custom-call | tf_op jit(solution)/shard_map/output/pallas_call | solution.py:469
  289.3 0.0 copy-start.4
  289.3 0.6 copy-done.4
  290.6 0.8 broadcast_in_dim.26.valid_ref
  291.4 25.3 %share_vectors.1 = bf16[8,256,128]{2,1,0:T(8,128)(2,1)} custom-call(bf16[256,128]{1,0:T(8,128)(2,1)} %copy-done.4, f32[256,128]{1,0:T(8,128)} %broadcast_in_dim.26.valid_ref), custom_call_target="tpu_custom_call" | custom-call | tf_op jit(solution)/shard_map/share_vectors/pallas_call | solution.py:534
  316.7 1.4 convolution_reduce_fusion
  318.1 0.1 reduce_sum.38
  318.2 0.0 copy-start.7
  318.3 0.6 exponential_reduce_fusion
  319.6 0.0 copy-done.8
  319.6 0.6 exponential_reduce_fusion.1
  320.9 0.6 multiply_reduce_fusion
  321.5 0.9 slice_bitcast_fusion
  322.4 0.7 slice_bitcast_fusion.1
  323.1 0.0 copy-done.7
  (2 shorter events, 0.0 us)
Async XLA Ops:
  6.9 2.9 copy-start.5
  15.5 144.9 %copy-start.2 = (f32[256,128]{1,0:T(8,128)S(1)}, f32[256,128]{1,0:T(8,128)}, u32[]{:S(2)}) copy-start(f32[256,128]{1,0:T(8,128)} %constant.31.clone.cos_ref) | copy-start | bytes 393220
  15.5 144.9 %copy-start.3 = (f32[256,128]{1,0:T(8,128)S(1)}, f32[256,128]{1,0:T(8,128)}, u32[]{:S(2)}) copy-start(f32[256,128]{1,0:T(8,128)} %constant.32.clone.sin_ref) | copy-start | bytes 393220
  160.5 17.6 %copy-start.6 = (bf16[2048]{0:T(1024)(128)(2,1)S(1)}, bf16[2048]{0:T(1024)(128)(2,1)}, u32[]{:S(2)}) copy-start(bf16[2048]{0:T(1024)(128)(2,1)} %param.18) | copy-start | bytes 12292
  160.5 17.6 %copy-start = (bf16[256,2048]{1,0:T(8,128)(2,1)S(1)}, bf16[256,2048]{1,0:T(8,128)(2,1)}, u32[]{:S(2)}) copy-start(bf16[256,2048]{1,0:T(8,128)(2,1)} %fusion.1.x_ref) | copy-start | bytes 3145732
  160.5 17.6 %copy-start.1 = (bf16[2048,128]{1,0:T(8,128)(2,1)S(1)}, bf16[2048,128]{1,0:T(8,128)(2,1)}, u32[]{:S(2)}) copy-start(bf16[2048,128]{1,0:T(8,128)(2,1)} %wv_ref.1) | copy-start | bytes 1572868
  178.1 141.5 %copy-start.8 = (f32[1,8]{1,0:T(1,128)S(1)}, f32[1,8]{1,0:T(1,128)}, u32[]{:S(2)}) copy-start(f32[1,8]{1,0:T(1,128)} %param.21) | copy-start | bytes 100
  289.3 0.6 copy-start.4
  318.2 4.9 %copy-start.7 = (f32[8]{0:T(128)}, f32[8]{0:T(128)S(1)}, u32[]{:S(2)}) copy-start(f32[8]{0:T(128)S(1)} %reduce_sum.38) | copy-start | bytes 100

commit v2 on v1

--- a/solution.py
+++ b/solution.py
@@ -225,46 +225,60 @@
 
 
 def gather_kernel(
-    x_ref, w_ref, wo_ref, xg, wg, wog,
-    local_sem, line_send, line_recv, core_send, core_recv, w_send, w_recv, wx_send, wx_recv, wo_send, wo_recv,
+    x_ref, wq_ref, wk_ref, wv_ref, xg, wg,
+    local_sem, line_send, line_recv, core_send, core_recv, w_send, w_recv, wx_send, wx_recv,
 ):
     z, x, t = place()
     d = z * 2 + x
     side = {"dp": z * 2 + 1 - x}
     partner = {"tensor": 1 - t}
     others = [lax.rem(z + o, 4) for o in range(4)]
+    origins = [lax.rem(z + 4 - o, 4) for o in range(4)]
     greet([{"dp": others[o] * 2 + x} for o in (1, 2, 3)] + [side, partner])
 
     line = Line(x_ref, lambda b: xg.at[b, t], line_send, line_recv, z, x)
-
-    def w_copy(o):
-        return remote(w_ref.at[others[o]], wg.at[d], w_send.at[o], w_recv.at[o], {"dp": others[o] * 2 + x})
+    sources = (wq_ref, wk_ref, wv_ref)
+    widths = [ref.shape[1] // 4 for ref in sources]
+    starts = [sum(widths[:i]) for i in range(3)]
+
+    def part(i, owner):
+        width = widths[i]
+        return sources[i].at[:, pl.ds(pl.multiple_of(owner * width, width), width)]
+
+    def slot_part(i, origin):
+        return wg.at[origin, :, pl.ds(starts[i], widths[i])]
+
+    def w_copy(o, i):
+        return remote(
+            part(i, others[o]), slot_part(i, d), w_send.at[o, i], w_recv.at[o, i], {"dp": others[o] * 2 + x}
+        )
+
+    def side_own(i):
+        return remote(part(i, z), slot_part(i, d), wx_send.at[0, i], wx_recv.at[0, i], side)
 
     def side_copy(o):
-        origin = lax.rem(z + 4 - o, 4)
-        slot = wg.at[origin * 2 + x]
-        return remote(w_ref.at[z] if o == 0 else slot, slot, wx_send.at[o], wx_recv.at[o], side)
+        slot = wg.at[origins[o] * 2 + x]
+        return remote(slot, slot, wx_send.at[o, 0], wx_recv.at[o, 0], side)
 
     def core_copy(block, own=False):
         slot = xg.at[block, t]
         return remote(x_ref if own else slot, slot, core_send.at[block], core_recv.at[block], partner)
 
     def w_receive(o):
-        origin = lax.rem(z + 4 - o, 4)
-        slot = wg.at[origin * 2 + x]
-        remote(slot, slot, w_send.at[o], w_recv.at[o], side).wait_recv()
+        for i in range(3):
+            slot = slot_part(i, origins[o] * 2 + x)
+            remote(slot, slot, w_send.at[o, i], w_recv.at[o, i], side).wait_recv()
         side_copy(o).start()
 
-    wo_copy = remote(wo_ref, wog.at[x], wo_send, wo_recv, side)
-    side_copy(0).start()
+    for o in (2, 1, 3):
+        for i in range(3):
+            w_copy(o, i).start()
+    for i in range(3):
+        side_own(i).start()
     line.send(0)
-    for o in (1, 3, 2):
-        w_copy(o).start()
     core_copy(z, own=True).start()
-    locals_ = [
-        pltpu.make_async_copy(x_ref, xg.at[z, t], local_sem.at[0]),
-        pltpu.make_async_copy(w_ref.at[z], wg.at[d], local_sem.at[1]),
-        pltpu.make_async_copy(wo_ref, wog.at[x], local_sem.at[2]),
+    locals_ = [pltpu.make_async_copy(x_ref, xg.at[z, t], local_sem.at[0])] + [
+        pltpu.make_async_copy(part(i, z), slot_part(i, d), local_sem.at[1 + i]) for i in range(3)
     ]
     for copy in locals_:
         copy.start()
@@ -273,49 +287,51 @@
     line.send(1)
     w_receive(1)
     w_receive(3)
-    wo_copy.start()
+    w_receive(2)
     line.receive(1, forward)
     line.send(2)
-    w_receive(2)
     line.receive(2, forward)
-    for o in range(4):
-        origin = lax.rem(z + 4 - o, 4)
-        slot = wg.at[origin * 2 + 1 - x]
-        remote(slot, slot, wx_send.at[o], wx_recv.at[o], side).wait_recv()
+    for i in range(3):
+        slot = slot_part(i, z * 2 + 1 - x)
+        remote(slot, slot, wx_send.at[0, i], wx_recv.at[0, i], side).wait_recv()
+    for o in (1, 2, 3):
+        slot = wg.at[origins[o] * 2 + 1 - x]
+        remote(slot, slot, wx_send.at[o, 0], wx_recv.at[o, 0], side).wait_recv()
     for block in range(4):
         slot = xg.at[block, 1 - t]
         remote(slot, slot, core_send.at[block], core_recv.at[block], partner).wait_recv()
-    remote(wog.at[1 - x], wog.at[1 - x], wo_send, wo_recv, side).wait_recv()
     for copy in locals_:
         copy.wait()
     line.finish()
     for o in (1, 2, 3):
-        w_copy(o).wait_send()
-    for o in range(4):
+        for i in range(3):
+            w_copy(o, i).wait_send()
         side_copy(o).wait_send()
-        core_copy(o).wait_send()
-    wo_copy.wait_send()
-
-
-def gather(x_block, w_parts, w_out):
+    for i in range(3):
+        side_own(i).wait_send()
+    for block in range(4):
+        core_copy(block).wait_send()
+
+
+def gather(x_block, w_query, key_matrix, value_matrix):
     dma = pltpu.SemaphoreType.DMA
     any_spec = pl.BlockSpec(memory_space=pl.ANY)
+    columns = (w_query.shape[1] + key_matrix.shape[1] + value_matrix.shape[1]) // 4
     return pl.pallas_call(
         gather_kernel,
         out_shape=(
             jax.ShapeDtypeStruct((4, 2) + x_block.shape, x_block.dtype),
-            jax.ShapeDtypeStruct((8,) + w_parts.shape[1:], w_parts.dtype),
-            jax.ShapeDtypeStruct((2,) + w_out.shape, w_out.dtype),
+            jax.ShapeDtypeStruct((8, w_query.shape[0], columns), w_query.dtype),
         ),
-        in_specs=[any_spec] * 3,
-        out_specs=(any_spec,) * 3,
+        in_specs=[any_spec] * 4,
+        out_specs=(any_spec,) * 2,
         scratch_shapes=[
-            dma((3,)), dma((2, 3)), dma((4,)), dma((4,)), dma((4,)),
-            dma((4,)), dma((4,)), dma((4,)), dma((4,)), dma, dma,
+            dma((4,)), dma((2, 3)), dma((4,)), dma((4,)), dma((4,)),
+            dma((4, 3)), dma((4, 3)), dma((4, 3)), dma((4, 3)),
         ],
         compiler_params=pltpu.CompilerParams(collective_id=1, has_side_effects=True),
         name="gather",
-    )(x_block, w_parts, w_out)
+    )(x_block, w_query, key_matrix, value_matrix)
 
 
 def attention_kernel(x_ref, w_ref, cos_ref, sin_ref, out_ref):
@@ -371,26 +387,35 @@
 
 
 def output_kernel(
-    a_ref, wo_ref, x_ref, gain_ref, wv_ref, updated_ref, partial_ref,
-    ag, term, other, total, branch,
-    line_send, line_recv, core_send, core_recv, row_send, row_recv,
+    a_ref, wo_in, x_ref, gain_ref, wv_ref, updated_ref, partial_ref,
+    ag, wog, term, other, total, branch, wo_sem, line_send, line_recv, core_send, core_recv, row_send, row_recv,
 ):
     z, x, t = place()
     partner = {"tensor": 1 - t}
     peers = [{"dp": lax.rem(z + o, 4) * 2 + x, "tensor": lax.rem(t + c, 2)} for o in range(4) for c in range(2)]
-    greet(peers[1:])
-    line = Line(a_ref, lambda b: ag.at[b], line_send, line_recv, z, x)
-    line.send(0)
+    side = {"dp": z * 2 + 1 - x}
+    greet(peers[1:] + [side])
+    lines = [
+        Line(a_ref.at[rb], lambda b, rb=rb: ag.at[b, rb], line_send.at[rb], line_recv.at[rb], z, x)
+        for rb in range(4)
+    ]
+    for line in lines:
+        line.send(0)
+    wo_copy = remote(wo_in, wog.at[x], wo_sem.at[0], wo_sem.at[1], side)
+    wo_copy.start()
+    wo_local = pltpu.make_async_copy(wo_in, wog.at[x], wo_sem.at[2])
+    wo_local.start()
     ag[pl.ds(z, 1)] = a_ref[...][None]
-    line.receive(0)
-    line.send(1)
-    line.receive(1)
-    line.send(2)
-    line.receive(2)
+    for step in (1, 2):
+        for line in lines:
+            line.receive(step - 1)
+            line.send(step)
+    wo_local.wait()
+    remote(wog.at[1 - x], wog.at[1 - x], wo_sem.at[0], wo_sem.at[1], side).wait_recv()
 
     half = ROWS // 2
     depth = a_ref.shape[2]
-    cols = wo_ref.shape[2]
+    cols = wo_in.shape[1]
     group = z // 2
     parity = lax.rem(z, 2)
 
@@ -403,32 +428,36 @@
             {"dp": rb * 2 + x, "tensor": group},
         )
 
-    blocks = [lax.rem(z + o, 4) for o in (1, 2, 3, 0)]
-    for o, rb in enumerate(blocks):
-        for side in range(2):
+    blocks = [0, 1, 2, 3]
+    mine = t == group
+
+    def reduce(rb):
+        core_copy(rb, rb).wait_recv()
+        summed = term[rb, t].astype(jnp.float32) + other[rb].astype(jnp.float32)
+        total[rb] = summed.astype(jnp.bfloat16)
+        here = mine & (z == rb)
+        pl.when(jnp.logical_not(here))(row_copy(rb, rb).start)
+
+        @pl.when(here)
+        def _():
+            branch[parity, t] = total[rb]
+
+    for rb in blocks:
+        lines[rb].receive(2)
+        for part_x in range(2):
             acc = jnp.zeros((ROWS, cols), jnp.float32)
             for part in range(4):
                 acc += jnp.dot(
-                    ag[part, rb], wo_ref[side, part * depth : (part + 1) * depth],
+                    ag[part, rb], wog[part_x, part * depth : (part + 1) * depth],
                     preferred_element_type=jnp.float32,
                 )
             rounded = acc.astype(jnp.bfloat16)
-            term[o, 0, :, side * cols : (side + 1) * cols] = rounded[:half]
-            term[o, 1, :, side * cols : (side + 1) * cols] = rounded[half:]
-        core_copy(o, rb).start()
-    mine = t == group
-    for o, rb in enumerate(blocks):
-        core_copy(o, rb).wait_recv()
-        summed = term[o, t].astype(jnp.float32) + other[o].astype(jnp.float32)
-        total[o] = summed.astype(jnp.bfloat16)
-        if o < 3:
-            row_copy(o, rb).start()
-        else:
-            pl.when(jnp.logical_not(mine))(row_copy(o, rb).start)
-
-            @pl.when(mine)
-            def _():
-                branch[parity, t] = total[o]
+            term[rb, 0, :, part_x * cols : (part_x + 1) * cols] = rounded[:half]
+            term[rb, 1, :, part_x * cols : (part_x + 1) * cols] = rounded[half:]
+        core_copy(rb, rb).start()
+        if rb > 0:
+            reduce(rb - 1)
+    reduce(3)
 
     for p in range(2):
         for h in range(2):
@@ -452,19 +481,17 @@
             scaled = (updated.astype(jnp.float32) * gain_ref[:, columns]).astype(jnp.bfloat16)
             partial += jnp.dot(scaled, wv_ref[columns], preferred_element_type=jnp.float32)
         partial_ref[rows] = partial.astype(jnp.bfloat16)
-    line.finish()
-    for o, rb in enumerate(blocks):
-        core_copy(o, rb).wait_send()
-        if o < 3:
-            row_copy(o, rb).wait_send()
-        else:
-            pl.when(jnp.logical_not(mine))(row_copy(o, rb).wait_send)
-
-
-def output(attended, wog, x_block, gain, w_vector):
+    wo_copy.wait_send()
+    for rb in blocks:
+        lines[rb].finish()
+        core_copy(rb, rb).wait_send()
+        pl.when(jnp.logical_not(mine & (z == rb)))(row_copy(rb, rb).wait_send)
+
+
+def output(attended, w_out, x_block, gain, w_vector):
     dma = pltpu.SemaphoreType.DMA
     bf16 = jnp.bfloat16
-    cols = 2 * wog.shape[2]
+    cols = 2 * w_out.shape[1]
     vmem = pl.BlockSpec(memory_space=pltpu.VMEM)
     return pl.pallas_call(
         output_kernel,
@@ -472,78 +499,160 @@
             jax.ShapeDtypeStruct(x_block.shape, bf16),
             jax.ShapeDtypeStruct((ROWS, VEC), bf16),
         ),
-        in_specs=[vmem] * 5,
+        in_specs=[vmem, pl.BlockSpec(memory_space=pl.ANY), vmem, vmem, vmem],
         out_specs=(vmem,) * 2,
         scratch_shapes=[
             pltpu.VMEM((4,) + attended.shape, bf16),
+            pltpu.VMEM((2,) + w_out.shape, bf16),
             pltpu.VMEM((4, 2, ROWS // 2, cols), bf16),
             pltpu.VMEM((4, ROWS // 2, cols), bf16),
             pltpu.VMEM((4, ROWS // 2, cols), bf16),
             pltpu.VMEM((2, 2, ROWS // 2, cols), bf16),
-            dma((2, 3)), dma((4,)), dma((4,)), dma((4,)), dma((4,)), dma((2, 2)),
+            dma((3,)), dma((4, 2, 3)), dma((4, 4)), dma((4,)), dma((4,)), dma((4,)), dma((2, 2)),
         ],
         compiler_params=pltpu.CompilerParams(
             collective_id=2, has_side_effects=True, vmem_limit_bytes=48 << 20
         ),
         name="output",
-    )(attended, wog, x_block, gain, w_vector)
-
-
-def vector_kernel(part_ref, valid_ref, all_ref, other, mine_buf, core_send, core_recv, send, recv):
+    )(attended, w_out, x_block, gain, w_vector)
+
+
+def score_kernel(
+    part_ref, length_ref, teacher_ref, score_ref, divergence_ref,
+    other, vectors_buf, queries, mine, arrived, core_sem, q_send, q_recv, s_send, s_recv,
+):
     dp, pipe, t = lax.axis_index("dp"), lax.axis_index("pipe"), lax.axis_index("tensor")
     partner = {"tensor": 1 - t}
     ring = [lax.rem(dp + o, 8) for o in range(8)]
-    pairs = [(o, p) for o in range(8) for p in range(2)][1:]
-    targets = [{"dp": ring[o], "pipe": lax.rem(pipe + p, 2)} for o, p in pairs]
-    greet([partner] + targets)
-    exchange = remote(part_ref, other, core_send, core_recv, partner)
+    barrier = pltpu.get_barrier_semaphore()
+
+    def signal(device):
+        pl.semaphore_signal(barrier, inc=1, device_id=device, device_id_type=MESH)
+
+    last = pipe == 1
+    itself = last & (t == 1)
+    signal(partner)
+    for o in range(8):
+        source = {"dp": ring[o], "pipe": 1, "tensor": pipe}
+        if o == 0:
+            pl.when(jnp.logical_not(itself))(lambda source=source: signal(source))
+        else:
+            signal(source)
+
+    @pl.when(last)
+    def _():
+        for o in range(1, 8):
+            signal({"dp": ring[o]})
+        pl.semaphore_wait(barrier, 24 - t)
+
+    @pl.when(jnp.logical_not(last))
+    def _():
+        pl.semaphore_wait(barrier, 1)
+
+    exchange = remote(part_ref, other, core_sem.at[0], core_sem.at[1], partner)
     exchange.start()
-    exchange.wait_recv()
-    projected = part_ref[...].astype(jnp.float32) + other[...].astype(jnp.float32)
-    vectors = projected * lax.rsqrt(jnp.sum(projected * projected, axis=1, keepdims=True) + vector_epsilon)
-    vectors = jnp.where(valid_ref[...] > 0.5, vectors, vectors[Q_ROWS : Q_ROWS + 1])
-    mine_buf[...] = vectors.astype(jnp.bfloat16)
-
-    def push(index):
-        return remote(mine_buf, all_ref.at[dp], send.at[index], recv.at[dp], targets[index])
-
-    @pl.when(pipe == 1)
+
+    @pl.when(last)
     def _():
-        for index in range(15):
-            push(index).start()
-        all_ref[pl.ds(dp, 1)] = mine_buf[...][None]
-
+        exchange.wait_recv()
+        projected = part_ref[...].astype(jnp.float32) + other[...].astype(jnp.float32)
+        vectors = projected * lax.rsqrt(
+            jnp.sum(projected * projected, axis=1, keepdims=True) + vector_epsilon
+        )
+        vectors_buf[...] = vectors.astype(jnp.bfloat16)
+        own = pl.ds(pl.multiple_of(t * QLEN, QLEN), QLEN)
+
+        def q_copy(o):
+            return remote(
+                vectors_buf.at[own], queries.at[dp], q_send.at[o], q_recv.at[dp], {"dp": ring[o]}
+            )
+
+        for o in range(1, 8):
+            q_copy(o).start()
+        queries[pl.ds(dp, 1)] = vectors_buf[own][None]
+        passage = vectors_buf[Q_ROWS:]
+        slot = lax.broadcasted_iota(jnp.int32, passage.shape, 0)
+        passage = jnp.where(
+            slot < length_ref[0], passage.astype(jnp.float32), passage[:1].astype(jnp.float32)
+        ).astype(jnp.bfloat16)
+        for o in range(1, 8):
+            ref = queries.at[ring[o]]
+            remote(ref, ref, q_send.at[o], q_recv.at[ring[o]], partner).wait_recv()
+        sims = lax.dot_general(
+            queries[...].reshape(8 * QLEN, VEC), passage, (((1,), (1,)), ((), ())),
+            preferred_element_type=jnp.float32,
+        )
+        best = jnp.broadcast_to(jnp.max(sims, axis=1, keepdims=True), (8 * QLEN, VEC))
+        mine[...] = jnp.sum(best.reshape(8, QLEN, VEC), axis=1)
+
+        def s_copy(o, c):
+            return remote(
+                mine, arrived.at[dp], s_send.at[o, c], s_recv.at[dp],
+                {"dp": ring[o], "pipe": t, "tensor": lax.rem(t + c, 2)},
+            )
+
+        first = s_copy(0, 0)
+        pl.when(jnp.logical_not(itself))(first.start)
+
+        @pl.when(itself)
+        def _():
+            arrived[pl.ds(dp, 1)] = mine[...][None]
+
+        rest = [(o, c) for o in range(8) for c in range(2)][1:]
+        for o, c in rest:
+            s_copy(o, c).start()
+        for o, c in rest:
+            s_copy(o, c).wait_send()
+        pl.when(jnp.logical_not(itself))(first.wait_send)
+        for o in range(1, 8):
+            q_copy(o).wait_send()
+
+    @pl.when(jnp.logical_not(last))
+    def _():
+        exchange.wait_recv()
+
+    exchange.wait_send()
     for o in range(8):
-        slot = all_ref.at[ring[o]]
-        wait = remote(slot, slot, send.at[0], recv.at[ring[o]], partner).wait_recv
+        ref = arrived.at[ring[o]]
+        wait = remote(ref, ref, s_send.at[0, 0], s_recv.at[ring[o]], partner).wait_recv
         if o == 0:
-            pl.when(pipe == 0)(wait)
+            pl.when(jnp.logical_not(itself))(wait)
         else:
             wait()
-    exchange.wait_send()
-
-    @pl.when(pipe == 1)
-    def _():
-        for index in range(15):
-            push(index).wait_send()
-
-
-def share_vectors(partial, valid):
+    lane = lax.broadcasted_iota(jnp.int32, (1, VEC), 1)
+    row = jnp.zeros((1, VEC), jnp.float32)
+    for p in range(8):
+        row = jnp.where(lane == p, arrived[p, pl.ds(dp, 1)], row)
+    student = row[:, :8]
+    score_ref[...] = student
+    teacher = teacher_ref[...]
+    log_student = student - jnp.log(jnp.sum(jnp.exp(student), axis=1, keepdims=True))
+    log_teacher = teacher - jnp.log(jnp.sum(jnp.exp(teacher), axis=1, keepdims=True))
+    divergence_ref[...] = jnp.sum(jnp.exp(log_teacher) * (log_teacher - log_student), axis=1, keepdims=True)
+
+
+def score(partial, lengths, teacher):
     dma = pltpu.SemaphoreType.DMA
     vmem = pl.BlockSpec(memory_space=pltpu.VMEM)
     return pl.pallas_call(
-        vector_kernel,
-        out_shape=jax.ShapeDtypeStruct((8, ROWS, VEC), jnp.bfloat16),
-        in_specs=[vmem] * 2,
-        out_specs=vmem,
+        score_kernel,
+        out_shape=(
+            jax.ShapeDtypeStruct(teacher.shape, jnp.float32),
+            jax.ShapeDtypeStruct((1, 1), jnp.float32),
+        ),
+        in_specs=[vmem, pl.BlockSpec(memory_space=pltpu.SMEM), vmem],
+        out_specs=(vmem,) * 2,
         scratch_shapes=[
             pltpu.VMEM((ROWS, VEC), jnp.bfloat16),
             pltpu.VMEM((ROWS, VEC), jnp.bfloat16),
-            dma, dma, dma((15,)), dma((8,)),
+            pltpu.VMEM((8, QLEN, VEC), jnp.bfloat16),
+            pltpu.VMEM((8, VEC), jnp.float32),
+            pltpu.VMEM((8, 8, VEC), jnp.float32),
+            dma((2,)), dma((8,)), dma((8,)), dma((8, 2)), dma((8,)),
         ],
         compiler_params=pltpu.CompilerParams(collective_id=3, has_side_effects=True),
-        name="share_vectors",
-    )(partial, valid)
+        name="score",
+    )(partial, lengths, teacher)
 
 
 def rope_tables():
@@ -565,32 +674,18 @@
     x_block = jnp.concatenate(
         [query_states[0], jnp.pad(passage_hidden_states[0], ((0, ROWS - Q_ROWS - PLEN), (0, 0)))], axis=0
     )
-    depth = w_query.shape[1]
-    w_parts = jnp.concatenate(
-        [array[0].reshape(depth, 4, -1).transpose(1, 0, 2) for array in (w_query, key_matrix, value_matrix)],
-        axis=2,
-    )
-    xg, wg, wog = gather(x_block, w_parts, w_out[0])
+    xg, wg = gather(x_block, w_query[0], key_matrix[0], value_matrix[0])
     cosine, sine = rope_tables()
     attended = attention(xg, wg.reshape(-1, wg.shape[2]), cosine, sine)
     updated, partial = output(
-        attended, wog, x_block, final_gain.astype(jnp.float32)[None, :], w_vector
-    )
-    slot = jnp.arange(ROWS) - Q_ROWS
-    valid = jnp.broadcast_to((slot < lengths[0])[:, None], (ROWS, VEC)).astype(jnp.float32)
-    vectors = share_vectors(partial, valid)
-    dp, pipe = lax.axis_index("dp"), lax.axis_index("pipe")
-    own = lax.dynamic_slice(vectors, (dp, pipe * QLEN, 0), (1, QLEN, VEC))[0]
-    sims = jnp.einsum("tc,psc->tps", own, vectors[:, Q_ROWS:], preferred_element_type=jnp.float32)
-    block = jnp.sum(jnp.max(sims, axis=2), axis=0)[None]
-    log_student = block - jnp.log(jnp.sum(jnp.exp(block), axis=1, keepdims=True))
-    log_teacher = teacher - jnp.log(jnp.sum(jnp.exp(teacher), axis=1, keepdims=True))
-    divergence = jnp.sum(jnp.exp(log_teacher) * (log_teacher - log_student), axis=1)
+        attended, w_out[0], x_block, final_gain.astype(jnp.float32)[None, :], w_vector
+    )
+    block, divergence = score(partial, lengths, teacher)
     return (
         updated[None, :Q_ROWS],
         updated[None, Q_ROWS : Q_ROWS + PLEN],
         block,
-        divergence,
+        divergence[0],
     )
 
 

time: 329 us -> 288 us (0.88); the launches traced: 323 us -> 288 us
  Pallas kernels: 299 us -> 279 us
  local copies, waits for them, and re-layouts: 13.7 us -> 2.79 us
  other arithmetic: 6.2 us -> 2.28 us
    pallas_call x1, Pallas kernels: 111 us -> 97.8 us  [output(): pl.pallas_call(output_kernel, out_shape=(jax.ShapeDtypeStruct(x_block.sha...]
    pallas_call x1, Pallas kernels: 25.3 us -> 17.8 us  [score(): pl.pallas_call(score_kernel, out_shape=(jax.ShapeDtypeStruct(teacher.shap...]
    unnamed x21 -> x15, local copies, waits for them, and re-layouts: 6.86 us -> 1.15 us
    another operation x3 -> x0, local copies, waits for them, and re-layouts: 4.42 us -> none  [by_heads(): array[0].reshape(depth, 4, -1).transpose(1, 0, 2)]
where the time goes in v2:
time: 288 us
  Pallas kernels  279 us (97%)
  between operations  3.17 us (1%)
    pallas_call x1, Pallas kernels, gather(): pl.pallas_call(gather_kernel, out_shape=(jax.ShapeDtypeStruct((4, 2) + x_...  146 us
    pallas_call x1, Pallas kernels, output(): pl.pallas_call(output_kernel, out_shape=(jax.ShapeDtypeStruct(x_block.sha...  97.8 us
    pallas_call x1, Pallas kernels, score(): pl.pallas_call(score_kernel, out_shape=(jax.ShapeDtypeStruct(teacher.shap...  17.8 us
    pallas_call x1, Pallas kernels, attention(): pl.pallas_call(attention_kernel, grid=(4,), out_shape=jax.ShapeDtypeStruc...  17.5 us

profile of v2, /device:TPU:0, one launch (start us, length us, event | category | flops | bytes accessed | tf_op | source)
XLA Modules:
  0.0 287.7 jit_solution(15628116922920253206)
XLA Ops:
  0.6 2.3 fusion.1.x_ref
  2.9 0.0 copy-start.3
  2.9 0.0 copy-start.4
  2.9 146.4 %gather.1 = (bf16[4,2,256,2048]{3,2,1,0:T(8,128)(2,1)}, bf16[8,512,768]{2,1,0:T(8,128)(2,1)}) custom-call(bf16[256,2048]{1,0:T(8,128)(2,1)} %fusion.1.x_ref, bf16[512,2048]{1,0:T(8,128)(2,1)} %bitcast.16, bf16[512,512]{1,0:T(8,128)(2,1)} %bitcast.18, bf16[512,512]{1,0:T(8,128)(2,1)} %bitcast.19), custom_call_target="tpu_custom_call" | custom-call | tf_op jit(solution)/shard_map/gather/pallas_call | solution.py:320
  149.3 0.0 copy-done.3
  149.3 0.0 copy-done.4
  149.3 0.0 copy-start.6
  149.3 0.0 copy-start
  149.3 0.0 copy-start.1
  149.3 0.0 copy-start.2
  149.4 17.5 %attention.1.a_ref = bf16[4,256,512]{2,1,0:T(8,128)(2,1)S(1)} custom-call(bf16[4,2,256,2048]{3,2,1,0:T(8,128)(2,1)} %get-tuple-element.10.x_ref, bf16[4096,768]{1,0:T(8,128)(2,1)} %bitcast.15, f32[256,128]{1,0:T(8,128)S(1)} %copy-done.3, f32[256,128]{1,0:T(8,128)S(1)} %copy-done.4), custom_call_target="tpu_custom_call" | custom-call | tf_op jit(solution)/shard_map/attention/pallas_call | solution.py:373
  166.9 0.0 copy-done.6
  166.9 0.0 copy-done
  166.9 0.0 copy-done.1
  167.0 0.0 copy-done.2
  167.0 97.8 %output.1 = (bf16[256,2048]{1,0:T(8,128)(2,1)S(1)}, bf16[256,128]{1,0:T(8,128)(2,1)S(1)}) custom-call(bf16[4,256,512]{2,1,0:T(8,128)(2,1)S(1)} %attention.1.a_ref, bf16[2048,512]{1,0:T(8,128)(2,1)S(1)} %bitcast.13, bf16[256,2048]{1,0:T(8,128)(2,1)S(1)} %copy-done, f32[1,2048]{1,0:T(1,128)S(1)} %bitcast.14, bf16[2048,128]{1,0:T(8,128)(2,1)S(1)} %copy-done.2), custom_call_target="tpu_custom_call" | custom-call | tf_op jit(solution)/shard_map/output/pallas_call | solution.py:496
  264.7 0.0 copy-start.5
  264.7 0.9 slice_bitcast_fusion
  265.7 0.7 slice_bitcast_fusion.1
  266.4 0.0 copy-done.5
  267.0 17.8 %score.1 = (f32[1,8]{1,0:T(1,128)}, f32[1,1]{1,0:T(1,128)}) custom-call(bf16[256,128]{1,0:T(8,128)(2,1)} %copy-done.5, s32[1]{0:T(128)S(6)} %copy.18.length_ref, f32[1,8]{1,0:T(1,128)} %teacher_ref.1), custom_call_target="tpu_custom_call" | custom-call | tf_op jit(solution)/shard_map/score/pallas_call | solution.py:637
  284.9 1.1 copy.19
  (1 shorter events, 0.0 us)
Async XLA Ops:
  2.9 146.4 %copy-start.3 = (f32[256,128]{1,0:T(8,128)S(1)}, f32[256,128]{1,0:T(8,128)}, u32[]{:S(2)}) copy-start(f32[256,128]{1,0:T(8,128)} %constant.7.clone.cos_ref) | copy-start | bytes 393220
  2.9 146.4 %copy-start.4 = (f32[256,128]{1,0:T(8,128)S(1)}, f32[256,128]{1,0:T(8,128)}, u32[]{:S(2)}) copy-start(f32[256,128]{1,0:T(8,128)} %constant.8.clone.sin_ref) | copy-start | bytes 393220
  149.3 17.6 %copy-start.6 = (bf16[2048]{0:T(1024)(128)(2,1)S(1)}, bf16[2048]{0:T(1024)(128)(2,1)}, u32[]{:S(2)}) copy-start(bf16[2048]{0:T(1024)(128)(2,1)} %param.18) | copy-start | bytes 12292
  149.3 17.6 %copy-start = (bf16[256,2048]{1,0:T(8,128)(2,1)S(1)}, bf16[256,2048]{1,0:T(8,128)(2,1)}, u32[]{:S(2)}) copy-start(bf16[256,2048]{1,0:T(8,128)(2,1)} %fusion.1.x_ref) | copy-start | bytes 3145732
  149.3 17.6 %copy-start.1 = (bf16[1,2048,512]{2,1,0:T(8,128)(2,1)S(1)}, bf16[1,2048,512]{2,1,0:T(8,128)(2,1)}, u32[]{:S(2)}) copy-start(bf16[1,2048,512]{2,1,0:T(8,128)(2,1)} %param.17) | copy-start | bytes 6291460
  149.3 17.6 %copy-start.2 = (bf16[2048,128]{1,0:T(8,128)(2,1)S(1)}, bf16[2048,128]{1,0:T(8,128)(2,1)}, u32[]{:S(2)}) copy-start(bf16[2048,128]{1,0:T(8,128)(2,1)} %wv_ref.1) | copy-start | bytes 1572868
  264.7 1.7 copy-start.5

commit v3 on v2

--- a/solution.py
+++ b/solution.py
@@ -236,7 +236,12 @@
     origins = [lax.rem(z + 4 - o, 4) for o in range(4)]
     greet([{"dp": others[o] * 2 + x} for o in (1, 2, 3)] + [side, partner])
 
-    line = Line(x_ref, lambda b: xg.at[b, t], line_send, line_recv, z, x)
+    height = ROWS // 4
+    cuts = [pl.ds(r * height, height) for r in range(4)]
+    lines = [
+        Line(x_ref.at[cut], lambda b, cut=cut: xg.at[b, t, cut], line_send.at[r], line_recv.at[r], z, x)
+        for r, cut in enumerate(cuts)
+    ]
     sources = (wq_ref, wk_ref, wv_ref)
     widths = [ref.shape[1] // 4 for ref in sources]
     starts = [sum(widths[:i]) for i in range(3)]
@@ -260,9 +265,10 @@
         slot = wg.at[origins[o] * 2 + x]
         return remote(slot, slot, wx_send.at[o, 0], wx_recv.at[o, 0], side)
 
-    def core_copy(block, own=False):
-        slot = xg.at[block, t]
-        return remote(x_ref if own else slot, slot, core_send.at[block], core_recv.at[block], partner)
+    def core_copy(block, r, own=False):
+        slot = xg.at[block, t, cuts[r]]
+        source = x_ref.at[cuts[r]] if own else slot
+        return remote(source, slot, core_send.at[block, r], core_recv.at[block, r], partner)
 
     def w_receive(o):
         for i in range(3):
@@ -270,27 +276,32 @@
             remote(slot, slot, w_send.at[o, i], w_recv.at[o, i], side).wait_recv()
         side_copy(o).start()
 
+    for line in lines:
+        line.send(0)
     for o in (2, 1, 3):
         for i in range(3):
             w_copy(o, i).start()
     for i in range(3):
         side_own(i).start()
-    line.send(0)
-    core_copy(z, own=True).start()
+    for r in range(4):
+        core_copy(z, r, own=True).start()
     locals_ = [pltpu.make_async_copy(x_ref, xg.at[z, t], local_sem.at[0])] + [
         pltpu.make_async_copy(part(i, z), slot_part(i, d), local_sem.at[1 + i]) for i in range(3)
     ]
     for copy in locals_:
         copy.start()
-    forward = lambda block: core_copy(block).start()
-    line.receive(0, forward)
-    line.send(1)
+    def advance(step):
+        for r, line in enumerate(lines):
+            line.receive(step, lambda block, r=r: core_copy(block, r).start())
+            if step < 2:
+                line.send(step + 1)
+
+    advance(0)
     w_receive(1)
     w_receive(3)
+    advance(1)
     w_receive(2)
-    line.receive(1, forward)
-    line.send(2)
-    line.receive(2, forward)
+    advance(2)
     for i in range(3):
         slot = slot_part(i, z * 2 + 1 - x)
         remote(slot, slot, wx_send.at[0, i], wx_recv.at[0, i], side).wait_recv()
@@ -298,11 +309,13 @@
         slot = wg.at[origins[o] * 2 + 1 - x]
         remote(slot, slot, wx_send.at[o, 0], wx_recv.at[o, 0], side).wait_recv()
     for block in range(4):
-        slot = xg.at[block, 1 - t]
-        remote(slot, slot, core_send.at[block], core_recv.at[block], partner).wait_recv()
+        for r in range(4):
+            slot = xg.at[block, 1 - t, cuts[r]]
+            remote(slot, slot, core_send.at[block, r], core_recv.at[block, r], partner).wait_recv()
     for copy in locals_:
         copy.wait()
-    line.finish()
+    for line in lines:
+        line.finish()
     for o in (1, 2, 3):
         for i in range(3):
             w_copy(o, i).wait_send()
@@ -310,7 +323,8 @@
     for i in range(3):
         side_own(i).wait_send()
     for block in range(4):
-        core_copy(block).wait_send()
+        for r in range(4):
+            core_copy(block, r).wait_send()
 
 
 def gather(x_block, w_query, key_matrix, value_matrix):
@@ -326,7 +340,7 @@
         in_specs=[any_spec] * 4,
         out_specs=(any_spec,) * 2,
         scratch_shapes=[
-            dma((4,)), dma((2, 3)), dma((4,)), dma((4,)), dma((4,)),
+            dma((4,)), dma((4, 2, 3)), dma((4, 4)), dma((4, 4)), dma((4, 4)),
             dma((4, 3)), dma((4, 3)), dma((4, 3)), dma((4, 3)),
         ],
         compiler_params=pltpu.CompilerParams(collective_id=1, has_side_effects=True),
@@ -334,9 +348,8 @@
     )(x_block, w_query, key_matrix, value_matrix)
 
 
-def attention_kernel(x_ref, w_ref, cos_ref, sin_ref, out_ref):
-    half = x_ref.shape[3]
-    first, second = x_ref[0, 0], x_ref[0, 1]
+def attend_block(first, second, w_ref, cos_ref, sin_ref, store):
+    half = first.shape[1]
     raw = jnp.dot(first, w_ref[:half], preferred_element_type=jnp.float32) + jnp.dot(
         second, w_ref[half:], preferred_element_type=jnp.float32
     )
@@ -363,49 +376,50 @@
         ) * HEAD_WIDTH ** (-0.5)
         weights = jnp.where(seen, jnp.exp(logits), 0.0)
         probability = (weights / jnp.sum(weights, axis=1, keepdims=True)).astype(jnp.bfloat16)
-        out_ref[0, :, head * HEAD_WIDTH : (head + 1) * HEAD_WIDTH] = jnp.dot(
-            probability, value, preferred_element_type=jnp.float32
-        ).astype(jnp.bfloat16)
-
-
-def attention(xg, weights, cosine, sine):
-    heads_cols = weights.shape[1] - 2 * HEAD_WIDTH
-    return pl.pallas_call(
-        attention_kernel,
-        grid=(4,),
-        out_shape=jax.ShapeDtypeStruct((4, ROWS, heads_cols), jnp.bfloat16),
-        in_specs=[
-            pl.BlockSpec((1,) + xg.shape[1:], lambda i: (i, 0, 0, 0)),
-            pl.BlockSpec(weights.shape, lambda i: (0, 0)),
-            pl.BlockSpec(cosine.shape, lambda i: (0, 0)),
-            pl.BlockSpec(sine.shape, lambda i: (0, 0)),
-        ],
-        out_specs=pl.BlockSpec((1, ROWS, heads_cols), lambda i: (i, 0, 0)),
-        compiler_params=pltpu.CompilerParams(vmem_limit_bytes=48 << 20),
-        name="attention",
-    )(xg, weights, cosine, sine)
+        store(
+            slice(head * HEAD_WIDTH, (head + 1) * HEAD_WIDTH),
+            jnp.dot(probability, value, preferred_element_type=jnp.float32).astype(jnp.bfloat16),
+        )
 
 
 def output_kernel(
-    a_ref, wo_in, x_ref, gain_ref, wv_ref, updated_ref, partial_ref,
-    ag, wog, term, other, total, branch, wo_sem, line_send, line_recv, core_send, core_recv, row_send, row_recv,
+    xg, w_in, wo_in, cos_ref, sin_ref, x_ref, gain_ref, wv_ref, updated_ref, partial_ref,
+    xs, w_all, load_sem, ag, wog, term, other, total, branch, wo_sem, line_send, line_recv, core_send, core_recv, row_send, row_recv,
 ):
     z, x, t = place()
     partner = {"tensor": 1 - t}
     peers = [{"dp": lax.rem(z + o, 4) * 2 + x, "tensor": lax.rem(t + c, 2)} for o in range(4) for c in range(2)]
     side = {"dp": z * 2 + 1 - x}
+    load_w = pltpu.make_async_copy(w_in, w_all, load_sem.at[4])
+    load_w.start()
+
+    def load_x(rb):
+        return pltpu.make_async_copy(xg.at[rb], xs.at[rb], load_sem.at[rb])
+
+    for rb in range(4):
+        load_x(rb).start()
     greet(peers[1:] + [side])
-    lines = [
-        Line(a_ref.at[rb], lambda b, rb=rb: ag.at[b, rb], line_send.at[rb], line_recv.at[rb], z, x)
-        for rb in range(4)
-    ]
-    for line in lines:
-        line.send(0)
     wo_copy = remote(wo_in, wog.at[x], wo_sem.at[0], wo_sem.at[1], side)
     wo_copy.start()
     wo_local = pltpu.make_async_copy(wo_in, wog.at[x], wo_sem.at[2])
     wo_local.start()
-    ag[pl.ds(z, 1)] = a_ref[...][None]
+
+    def line_of(rb):
+        return Line(ag.at[z, rb], lambda b: ag.at[b, rb], line_send.at[rb], line_recv.at[rb], z, x)
+
+    load_w.wait()
+
+    @pl.loop(0, 4)
+    def _(rb):
+        load_x(rb).wait()
+
+        def store(columns, values):
+            ag[pl.ds(z, 1), pl.ds(rb, 1), :, columns] = values[None, None]
+
+        attend_block(xs[rb, 0], xs[rb, 1], w_all, cos_ref, sin_ref, store)
+        line_of(rb).send(0)
+
+    lines = [line_of(rb) for rb in range(4)]
     for step in (1, 2):
         for line in lines:
             line.receive(step - 1)
@@ -414,7 +428,7 @@
     remote(wog.at[1 - x], wog.at[1 - x], wo_sem.at[0], wo_sem.at[1], side).wait_recv()
 
     half = ROWS // 2
-    depth = a_ref.shape[2]
+    depth = ag.shape[3]
     cols = wo_in.shape[1]
     group = z // 2
     parity = lax.rem(z, 2)
@@ -488,7 +502,7 @@
         pl.when(jnp.logical_not(mine & (z == rb)))(row_copy(rb, rb).wait_send)
 
 
-def output(attended, w_out, x_block, gain, w_vector):
+def output(xg, weights, w_out, cosine, sine, x_block, gain, w_vector):
     dma = pltpu.SemaphoreType.DMA
     bf16 = jnp.bfloat16
     cols = 2 * w_out.shape[1]
@@ -499,10 +513,13 @@
             jax.ShapeDtypeStruct(x_block.shape, bf16),
             jax.ShapeDtypeStruct((ROWS, VEC), bf16),
         ),
-        in_specs=[vmem, pl.BlockSpec(memory_space=pl.ANY), vmem, vmem, vmem],
+        in_specs=[pl.BlockSpec(memory_space=pl.ANY)] * 3 + [vmem] * 5,
         out_specs=(vmem,) * 2,
         scratch_shapes=[
-            pltpu.VMEM((4,) + attended.shape, bf16),
+            pltpu.VMEM(xg.shape, bf16),
+            pltpu.VMEM(weights.shape, bf16),
+            dma((5,)),
+            pltpu.VMEM((4, 4, ROWS, weights.shape[1] - 2 * HEAD_WIDTH), bf16),
             pltpu.VMEM((2,) + w_out.shape, bf16),
             pltpu.VMEM((4, 2, ROWS // 2, cols), bf16),
             pltpu.VMEM((4, ROWS // 2, cols), bf16),
@@ -514,7 +531,7 @@
             collective_id=2, has_side_effects=True, vmem_limit_bytes=48 << 20
         ),
         name="output",
-    )(attended, w_out, x_block, gain, w_vector)
+    )(xg, weights, w_out, cosine, sine, x_block, gain, w_vector)
 
 
 def score_kernel(
@@ -676,9 +693,9 @@
     )
     xg, wg = gather(x_block, w_query[0], key_matrix[0], value_matrix[0])
     cosine, sine = rope_tables()
-    attended = attention(xg, wg.reshape(-1, wg.shape[2]), cosine, sine)
     updated, partial = output(
-        attended, w_out[0], x_block, final_gain.astype(jnp.float32)[None, :], w_vector
+        xg, wg.reshape(-1, wg.shape[2]), w_out[0], cosine, sine, x_block,
+        final_gain.astype(jnp.float32)[None, :], w_vector,
     )
     block, divergence = score(partial, lengths, teacher)
     return (

time: 288 us -> 276 us (0.958)
  Pallas kernels: 279 us -> 266 us
    pallas_call x1, Pallas kernels: 97.8 us -> 120 us  [output(): pl.pallas_call(output_kernel, out_shape=(jax.ShapeDtypeStruct(x_block.sha...]
    pallas_call x1, Pallas kernels: 146 us -> 128 us  [gather(): pl.pallas_call(gather_kernel, out_shape=(jax.ShapeDtypeStruct((4, 2) + x_...]
    pallas_call x1 -> x0, Pallas kernels: 17.5 us -> none  [attention(): pl.pallas_call(attention_kernel, grid=(4,), out_shape=jax.ShapeDtypeStruc...]
where the time goes in v3:
time: 276 us; the launch traced here: 275 us
  Pallas kernels  266 us (96%)
  local copies, waits for them, and re-layouts  3.82 us (1%)
  between operations  3.15 us (1%)
    pallas_call x1, Pallas kernels, gather(): pl.pallas_call(gather_kernel, out_shape=(jax.ShapeDtypeStruct((4, 2) + x_...  128 us
    pallas_call x1, Pallas kernels, output(): pl.pallas_call(output_kernel, out_shape=(jax.ShapeDtypeStruct(x_block.sha...  120 us
    pallas_call x1, Pallas kernels, score(): pl.pallas_call(score_kernel, out_shape=(jax.ShapeDtypeStruct(teacher.shap...  17.8 us

profile of v3, /device:TPU:0, one launch (start us, length us, event | category | flops | bytes accessed | tf_op | source)
XLA Modules:
  0.0 275.3 jit_solution(5418682571759232706)
XLA Ops:
  0.6 2.3 fusion.1.x_ref
  2.9 0.0 copy-start.6
  2.9 0.0 copy-start
  2.9 0.0 copy-start.1
  2.9 0.0 copy-start.3
  2.9 0.0 copy-start.4
  2.9 127.8 %gather.1 = (bf16[4,2,256,2048]{3,2,1,0:T(8,128)(2,1)}, bf16[8,512,768]{2,1,0:T(8,128)(2,1)}) custom-call(bf16[256,2048]{1,0:T(8,128)(2,1)} %fusion.1.x_ref, bf16[512,2048]{1,0:T(8,128)(2,1)} %bitcast.16, bf16[512,512]{1,0:T(8,128)(2,1)} %bitcast.18, bf16[512,512]{1,0:T(8,128)(2,1)} %bitcast.19), custom_call_target="tpu_custom_call" | custom-call | tf_op jit(solution)/shard_map/gather/pallas_call | solution.py:334
  130.8 0.0 copy-done.6
  130.8 0.0 copy-done
  130.8 0.0 copy-done.1
  130.8 0.0 copy-done.3
  130.8 0.0 copy-done.4
  130.8 0.0 copy-start.2
  130.8 1.0 copy-done.2
  131.9 120.4 %output.1 = (bf16[256,2048]{1,0:T(8,128)(2,1)S(1)}, bf16[256,128]{1,0:T(8,128)(2,1)S(1)}) custom-call(bf16[4,2,256,2048]{3,2,1,0:T(8,128)(2,1)} %get-tuple-element.10.xg, bf16[4096,768]{1,0:T(8,128)(2,1)} %bitcast.15, bf16[2048,512]{1,0:T(8,128)(2,1)S(1)} %bitcast.13, f32[256,128]{1,0:T(8,128)S(1)} %copy-done.3, f32[256,128]{1,0:T(8,128)S(1)} %copy-done.4, ...), custom_call_target="tpu_custom_call" | custom-call | tf_op jit(solution)/shard_map/output/pallas_call | solution.py:510
  252.3 0.0 copy-start.5
  252.3 0.9 slice_bitcast_fusion
  253.2 0.7 slice_bitcast_fusion.1
  253.9 0.0 copy-done.5
  254.6 17.8 %score.1 = (f32[1,8]{1,0:T(1,128)}, f32[1,1]{1,0:T(1,128)}) custom-call(bf16[256,128]{1,0:T(8,128)(2,1)} %copy-done.5, s32[1]{0:T(128)S(6)} %copy.18.length_ref, f32[1,8]{1,0:T(1,128)} %teacher_ref.1), custom_call_target="tpu_custom_call" | custom-call | tf_op jit(solution)/shard_map/score/pallas_call | solution.py:654
  272.4 1.1 copy.19
  (1 shorter events, 0.0 us)
Async XLA Ops:
  2.9 127.9 %copy-start.6 = (bf16[2048]{0:T(1024)(128)(2,1)S(1)}, bf16[2048]{0:T(1024)(128)(2,1)}, u32[]{:S(2)}) copy-start(bf16[2048]{0:T(1024)(128)(2,1)} %param.18) | copy-start | bytes 12292
  2.9 127.9 %copy-start = (bf16[256,2048]{1,0:T(8,128)(2,1)S(1)}, bf16[256,2048]{1,0:T(8,128)(2,1)}, u32[]{:S(2)}) copy-start(bf16[256,2048]{1,0:T(8,128)(2,1)} %fusion.1.x_ref) | copy-start | bytes 3145732
  2.9 127.9 %copy-start.1 = (bf16[1,2048,512]{2,1,0:T(8,128)(2,1)S(1)}, bf16[1,2048,512]{2,1,0:T(8,128)(2,1)}, u32[]{:S(2)}) copy-start(bf16[1,2048,512]{2,1,0:T(8,128)(2,1)} %param.17) | copy-start | bytes 6291460
  2.9 127.9 %copy-start.3 = (f32[256,128]{1,0:T(8,128)S(1)}, f32[256,128]{1,0:T(8,128)}, u32[]{:S(2)}) copy-start(f32[256,128]{1,0:T(8,128)} %constant.7.clone.cos_ref) | copy-start | bytes 393220
  2.9 127.9 %copy-start.4 = (f32[256,128]{1,0:T(8,128)S(1)}, f32[256,128]{1,0:T(8,128)}, u32[]{:S(2)}) copy-start(f32[256,128]{1,0:T(8,128)} %constant.8.clone.sin_ref) | copy-start | bytes 393220
  130.8 1.0 copy-start.2
  252.3 1.7 copy-start.5

commit v4 on v3

--- a/solution.py
+++ b/solution.py
@@ -384,7 +384,7 @@
 
 def output_kernel(
     xg, w_in, wo_in, cos_ref, sin_ref, x_ref, gain_ref, wv_ref, updated_ref, partial_ref,
-    xs, w_all, load_sem, ag, wog, term, other, total, branch, wo_sem, line_send, line_recv, core_send, core_recv, row_send, row_recv,
+    xs, w_all, load_sem, ag, wog, term, other, total, branch, wo_sem, wo_send, wo_recv, line_send, line_recv, core_send, core_recv, row_send, row_recv,
 ):
     z, x, t = place()
     partner = {"tensor": 1 - t}
@@ -399,9 +399,13 @@
     for rb in range(4):
         load_x(rb).start()
     greet(peers[1:] + [side])
-    wo_copy = remote(wo_in, wog.at[x], wo_sem.at[0], wo_sem.at[1], side)
-    wo_copy.start()
-    wo_local = pltpu.make_async_copy(wo_in, wog.at[x], wo_sem.at[2])
+    wo_rows = wo_in.shape[0] // 8
+
+    def wo_copy(k):
+        cut = pl.ds(pl.multiple_of(k * wo_rows, wo_rows), wo_rows)
+        return remote(wo_in.at[cut], wog.at[x, cut], wo_send.at[k], wo_recv.at[k], side)
+
+    wo_local = pltpu.make_async_copy(wo_in, wog.at[x], wo_sem)
     wo_local.start()
 
     def line_of(rb):
@@ -418,14 +422,19 @@
 
         attend_block(xs[rb, 0], xs[rb, 1], w_all, cos_ref, sin_ref, store)
         line_of(rb).send(0)
+        wo_copy(rb).start()
 
     lines = [line_of(rb) for rb in range(4)]
     for step in (1, 2):
-        for line in lines:
+        for rb, line in enumerate(lines):
             line.receive(step - 1)
             line.send(step)
+            if step == 1:
+                wo_copy(4 + rb).start()
     wo_local.wait()
-    remote(wog.at[1 - x], wog.at[1 - x], wo_sem.at[0], wo_sem.at[1], side).wait_recv()
+    for k in range(8):
+        arriving = wog.at[1 - x, pl.ds(k * wo_rows, wo_rows)]
+        remote(arriving, arriving, wo_send.at[k], wo_recv.at[k], side).wait_recv()
 
     half = ROWS // 2
     depth = ag.shape[3]
@@ -495,7 +504,8 @@
             scaled = (updated.astype(jnp.float32) * gain_ref[:, columns]).astype(jnp.bfloat16)
             partial += jnp.dot(scaled, wv_ref[columns], preferred_element_type=jnp.float32)
         partial_ref[rows] = partial.astype(jnp.bfloat16)
-    wo_copy.wait_send()
+    for k in range(8):
+        wo_copy(k).wait_send()
     for rb in blocks:
         lines[rb].finish()
         core_copy(rb, rb).wait_send()
@@ -525,7 +535,7 @@
             pltpu.VMEM((4, ROWS // 2, cols), bf16),
             pltpu.VMEM((4, ROWS // 2, cols), bf16),
             pltpu.VMEM((2, 2, ROWS // 2, cols), bf16),
-            dma((3,)), dma((4, 2, 3)), dma((4, 4)), dma((4,)), dma((4,)), dma((4,)), dma((2, 2)),
+            dma, dma((8,)), dma((8,)), dma((4, 2, 3)), dma((4, 4)), dma((4,)), dma((4,)), dma((4,)), dma((2, 2)),
         ],
         compiler_params=pltpu.CompilerParams(
             collective_id=2, has_side_effects=True, vmem_limit_bytes=48 << 20

time: 276 us -> 276 us (level)
  no operation moved by 1% of the time
where the time goes in v4:
time: 276 us; the launch traced here: 275 us
  Pallas kernels  266 us (96%)
  local copies, waits for them, and re-layouts  3.82 us (1%)
  between operations  3.15 us (1%)
    pallas_call x1, Pallas kernels, gather(): pl.pallas_call(gather_kernel, out_shape=(jax.ShapeDtypeStruct((4, 2) + x_...  128 us
    pallas_call x1, Pallas kernels, output(): pl.pallas_call(output_kernel, out_shape=(jax.ShapeDtypeStruct(x_block.sha...  121 us
    pallas_call x1, Pallas kernels, score(): pl.pallas_call(score_kernel, out_shape=(jax.ShapeDtypeStruct(teacher.shap...  17.8 us

profile of v4, /device:TPU:0, one launch (start us, length us, event | category | flops | bytes accessed | tf_op | source)
XLA Modules:
  0.0 275.4 jit_solution(5869513441169930688)
XLA Ops:
  0.6 2.3 fusion.1.x_ref
  2.9 0.0 copy-start.6
  2.9 0.0 copy-start
  2.9 0.0 copy-start.1
  2.9 0.0 copy-start.3
  2.9 0.0 copy-start.4
  2.9 127.8 %gather.1 = (bf16[4,2,256,2048]{3,2,1,0:T(8,128)(2,1)}, bf16[8,512,768]{2,1,0:T(8,128)(2,1)}) custom-call(bf16[256,2048]{1,0:T(8,128)(2,1)} %fusion.1.x_ref, bf16[512,2048]{1,0:T(8,128)(2,1)} %bitcast.16, bf16[512,512]{1,0:T(8,128)(2,1)} %bitcast.18, bf16[512,512]{1,0:T(8,128)(2,1)} %bitcast.19), custom_call_target="tpu_custom_call" | custom-call | tf_op jit(solution)/shard_map/gather/pallas_call | solution.py:334
  130.8 0.0 copy-done.6
  130.8 0.0 copy-done
  130.8 0.0 copy-done.1
  130.8 0.0 copy-done.3
  130.8 0.0 copy-done.4
  130.8 0.0 copy-start.2
  130.8 1.0 copy-done.2
  131.9 120.5 %output.1 = (bf16[256,2048]{1,0:T(8,128)(2,1)S(1)}, bf16[256,128]{1,0:T(8,128)(2,1)S(1)}) custom-call(bf16[4,2,256,2048]{3,2,1,0:T(8,128)(2,1)} %get-tuple-element.10.xg, bf16[4096,768]{1,0:T(8,128)(2,1)} %bitcast.15, bf16[2048,512]{1,0:T(8,128)(2,1)S(1)} %bitcast.13, f32[256,128]{1,0:T(8,128)S(1)} %copy-done.3, f32[256,128]{1,0:T(8,128)S(1)} %copy-done.4, ...), custom_call_target="tpu_custom_call" | custom-call | tf_op jit(solution)/shard_map/output/pallas_call | solution.py:520
  252.4 0.0 copy-start.5
  252.4 0.9 slice_bitcast_fusion
  253.3 0.7 slice_bitcast_fusion.1
  254.1 0.0 copy-done.5
  254.7 17.8 %score.1 = (f32[1,8]{1,0:T(1,128)}, f32[1,1]{1,0:T(1,128)}) custom-call(bf16[256,128]{1,0:T(8,128)(2,1)} %copy-done.5, s32[1]{0:T(128)S(6)} %copy.18.length_ref, f32[1,8]{1,0:T(1,128)} %teacher_ref.1), custom_call_target="tpu_custom_call" | custom-call | tf_op jit(solution)/shard_map/score/pallas_call | solution.py:664
  272.5 1.1 copy.19
  (1 shorter events, 0.0 us)
Async XLA Ops:
  2.9 127.9 %copy-start.6 = (bf16[2048]{0:T(1024)(128)(2,1)S(1)}, bf16[2048]{0:T(1024)(128)(2,1)}, u32[]{:S(2)}) copy-start(bf16[2048]{0:T(1024)(128)(2,1)} %param.18) | copy-start | bytes 12292
  2.9 127.9 %copy-start = (bf16[256,2048]{1,0:T(8,128)(2,1)S(1)}, bf16[256,2048]{1,0:T(8,128)(2,1)}, u32[]{:S(2)}) copy-start(bf16[256,2048]{1,0:T(8,128)(2,1)} %fusion.1.x_ref) | copy-start | bytes 3145732
  2.9 127.9 %copy-start.1 = (bf16[1,2048,512]{2,1,0:T(8,128)(2,1)S(1)}, bf16[1,2048,512]{2,1,0:T(8,128)(2,1)}, u32[]{:S(2)}) copy-start(bf16[1,2048,512]{2,1,0:T(8,128)(2,1)} %param.17) | copy-start | bytes 6291460
  2.9 127.9 %copy-start.3 = (f32[256,128]{1,0:T(8,128)S(1)}, f32[256,128]{1,0:T(8,128)}, u32[]{:S(2)}) copy-start(f32[256,128]{1,0:T(8,128)} %constant.7.clone.cos_ref) | copy-start | bytes 393220
  2.9 127.9 %copy-start.4 = (f32[256,128]{1,0:T(8,128)S(1)}, f32[256,128]{1,0:T(8,128)}, u32[]{:S(2)}) copy-start(f32[256,128]{1,0:T(8,128)} %constant.8.clone.sin_ref) | copy-start | bytes 393220
  130.8 1.0 copy-start.2
  252.4 1.7 copy-start.5
